TPU v7x, 1024 devices: a whole 4x4x32 slice. The times are simulated.
1024 devices in a mesh: fsdp: 128 (over y_hi, z, core), replica: 8 (over y_lo, x).
Axes of the slice: x: 4, y: 4 (y_hi: 2, y_lo: 2; y = y_hi * 2 + y_lo), z: 32, core: 2. Of those that a mesh axis runs over, the one named last changes fastest.
Arguments:
- tokens: bfloat16 [8, 16384, 4096], P('replica', 'fsdp'), may hold values from -18 to 18
- norm_gain: bfloat16 [8, 4096], P('replica'), may hold values from 0.5 to 1.5
- weight: bfloat16 [8, 4096, 512], P('replica', 'fsdp'), may hold values from -1 to 1
- cotangent: bfloat16 [8, 16384, 512], P('replica', 'fsdp'), may hold values from -8 to 8
- global_params: float32 [16, 1048576], P(None, 'fsdp'), may hold values from -6 to 6
- local_params: float32 [8, 16, 1048576], P('replica', None, 'fsdp'), may hold values from -6 to 6
- momentum: float32 [16, 1048576], P(None, 'fsdp'), may hold values from -6 to 6
- fragment: int32 [1], replicated, may hold values from 0 to 15
Outputs:
- projected: bfloat16 [8, 16384, 512], P('replica', 'fsdp')
- token_grad: bfloat16 [8, 16384, 4096], P('replica', 'fsdp')
- global_next: float32 [1048576], P('fsdp')
- momentum_next: float32 [1048576], P('fsdp')
All inputs are finite; a program needn't handle non-finite values.
Results may differ from a plain program's by a relative error of at most 0.0049.
Values may be sent and summed in bfloat16 or wider, within the bound.
No kernel may reach another device: no remote copies, remote signals or barrier semaphores. Data moves between devices by JAX's collectives and lax.ppermute only.
A program may use at most 32 MiB of HBM per device.

v0:
```python
import jax
import jax.numpy as jnp
from jax import lax
from jax.sharding import PartitionSpec as P

epsilon = 1e-05
outer_momentum = 0.9
outer_rate = 0.7


def shards(tokens, norm_gain, weight, cotangent, global_params, local_params, momentum, fragment):
    floated = tokens[0].astype(jnp.float32)
    inv_rms = lax.rsqrt(jnp.mean(floated * floated, axis=1, keepdims=True) + epsilon)
    unit_rows = floated * inv_rms
    gain_row = norm_gain[0].astype(jnp.float32)
    normed = (unit_rows * gain_row).astype(jnp.bfloat16)
    upstream = cotangent[0]
    full_weight = lax.all_gather(weight, "fsdp", axis=1, tiled=True)[0]
    forward_sum = jnp.dot(normed, full_weight, preferred_element_type=jnp.float32)
    grad_normed = lax.dot_general(
        upstream, full_weight, (((1,), (1,)), ((), ())), preferred_element_type=jnp.float32
    )
    projected = forward_sum.astype(jnp.bfloat16)[None]
    gained = grad_normed * gain_row
    inner_mean = jnp.mean(gained * unit_rows, axis=1, keepdims=True)
    token_grad = (inv_rms * (gained - unit_rows * inner_mean)).astype(jnp.bfloat16)[None]
    chosen = fragment[0]
    global_row = lax.dynamic_index_in_dim(global_params, chosen, 0, keepdims=False)
    moment_row = lax.dynamic_index_in_dim(momentum, chosen, 0, keepdims=False)
    local_row = lax.dynamic_index_in_dim(local_params[0], chosen, 0, keepdims=False)
    difference = global_row - local_row
    replica_count = lax.axis_size("replica")
    summed = lax.psum(difference, "replica")
    pseudo = summed / replica_count
    momentum_next = outer_momentum * moment_row + pseudo
    global_next = global_row - outer_rate * (pseudo + outer_momentum * momentum_next)
    return (projected, token_grad, global_next, momentum_next)


def solution(mesh):
    placed = (
        P("replica", "fsdp", None),
        P("replica", None),
        P("replica", "fsdp", None),
        P("replica", "fsdp", None),
        P(None, "fsdp"),
        P("replica", None, "fsdp"),
        P(None, "fsdp"),
        P(),
    )
    return jax.shard_map(
        shards,
        mesh=mesh,
        in_specs=placed,
        out_specs=(P("replica", "fsdp", None), P("replica", "fsdp", None), P("fsdp"), P("fsdp")),
        check_vma=False,
    )
```

profile of v0, /device:TPU:1, one launch (start us, length us, event | category | flops | bytes accessed | tf_op | source)
XLA Modules:
  0.0 313.6 jit_solution(9556604341936484113)
XLA Ops:
  7.2 0.0 copy-start
  7.2 0.0 copy-start.1
  7.2 0.0 all-gather.2.cloned.1.call-start
  7.2 0.7 all-gather.2.cloned.1.call-update
  7.9 0.7 mul.89
  9.3 0.0 copy-done
  9.4 1.0 constant_dynamic-slice_fusion
  10.4 28.1 %psum.7 = f32[8192]{0:T(1024)S(1)} all-reduce(f32[8192]{0:T(1024)S(1)} %sub.10), channel_id=1, replica_groups=mesh['fsdp'=128,'replica'=8] {'replica'}, use_global_device_ids=true, to_apply=%region_2.3 | all-reduce | flops 8192 | bytes 65536 | tf_op jit(solution)/shard_map/psum | solution.py:33
  38.4 1.5 fusion.11
  40.0 1.0 dynamic-slice_multiply_fusion
  41.0 0.6 multiply_subtract_fusion
  41.6 257.3 %all-gather.2.cloned.1.call-done = bf16[1,4096,512]{2,1,0:T(8,128)(2,1)} async-done(((bf16[1,32,512]{2,1,0:T(8,128)(2,1)}), bf16[1,4096,512]{2,1,0:T(8,128)(2,1)}) %all-gather.2.cloned.1.call-update) | async-done | bytes 4194320 | tf_op jit(solution)/shard_map/all_gather | solution.py:18
  298.9 0.0 copy-done.1
  298.9 3.8 %fusion.7 = (f32[128]{0:T(128)S(1)}, f32[128,4096]{1,0:T(8,128)S(1)}) fusion(bf16[1,128,4096]{2,1,0:T(8,128)(2,1)S(1)} %copy-done.1, f32[128]{0:T(128)S(1)} %add_rsqrt_fusion, f32[4096]{0:T(1024)S(1)} %bitcast.57, bf16[1,4096,512]{2,1,0:T(8,128)(2,1)} %all-gather.2.cloned.1.call-done, bf16[1,128,512]{2,1,0:T(8,128)(2,1)} %param.11), kind=kOutput, calls=%fused_computation.10 | convolution fusion | flops 539492224 | bytes 7488512 | tf_op jit(solution)/shard_map/dot_general | solution.py:20
  302.7 0.0 copy-start.2
  302.8 1.5 fusion.22
  304.2 1.1 copy-done.2
  305.3 1.4 fusion.17
  (4 shorter events, 0.1 us)
Async XLA Ops:
  7.2 2.2 copy-start
  7.2 291.7 %copy-start.1 = (bf16[1,128,4096]{2,1,0:T(8,128)(2,1)S(1)}, bf16[1,128,4096]{2,1,0:T(8,128)(2,1)}, u32[]{:S(2)}) copy-start(bf16[1,128,4096]{2,1,0:T(8,128)(2,1)} %param.8) | copy-start | bytes 3145732
  7.2 291.7 %all-gather.2.cloned.1.call-start = ((), (), s32[]{:S(2)}) async-start(), calls=%async_computation | async-start | bytes 4227072 | tf_op jit(solution)/shard_map/all_gather | solution.py:18
  302.7 2.6 copy-start.2
Sparse Core Ops, SparseCore 0:
  12.5 286.3 all-gather.1
where the time goes:
time: 314 us
  waiting for transfers between devices  258 us (82%)
  blocking collectives  28.1 us (9%)
  between operations  14.7 us (5%)
  other arithmetic  5.37 us (2%)
  matrix products  5.26 us (2%)
    all_gather x1, waiting for transfers between devices, shards(): full_weight = lax.all_gather(weight, 'fsdp', axis=1, tiled=True)[0]  257 us
    psum x1, blocking collectives, shards(): summed = lax.psum(difference, 'replica')  28.1 us
  transfers between devices with their start and end apart: 1, of which 1 were waited for; matrix products, arithmetic and copies ran while one was open for 2% of the time, Pallas kernels for 0%

commit v1 on v0

v1 whole, which is shorter than its diff:
```python
import functools

import jax
import jax.numpy as jnp
from jax import lax
from jax.experimental import pallas as pl
from jax.experimental.pallas import tpu as pltpu
from jax.sharding import PartitionSpec as P

epsilon = 1e-05
outer_momentum = 0.9
outer_rate = 0.7

Y, Z, C = 2, 32, 2
HOPS = (16, 8, 4, 2, 1)


def at(y, z, c):
    return (y * Z + z % Z) * C + c


def pairs(step):
    return [
        (at(y, z, c), at(*step(y, z, c)))
        for y in range(Y)
        for z in range(Z)
        for c in range(C)
    ]


def along_z(array, hop):
    return lax.ppermute(array, "fsdp", pairs(lambda y, z, c: (y, z + (hop if c == 0 else -hop), c)))


def across_y(array):
    return lax.ppermute(array, "fsdp", pairs(lambda y, z, c: (1 - y, z, c)))


def across_core(array):
    return lax.ppermute(array, "fsdp", pairs(lambda y, z, c: (y, z, 1 - c)))


def offset(slot, hops):
    return sum(hop for bit, hop in enumerate(hops) if slot >> bit & 1)


def layer_kernel(rows, layout, *refs):
    pieces = refs[: len(layout)]
    tokens, inv, gain, upstream, projected, token_grad, full, sem = refs[len(layout) :]
    place = lax.axis_index("fsdp")
    core = lax.rem(place, C)
    chip = lax.div(place, C)
    z, y = lax.rem(chip, Z), lax.div(chip, Z)
    for piece, (other_y, other_core, offsets) in zip(pieces, layout):
        owner_y = 1 - y if other_y else y
        owner_core = 1 - core if other_core else core
        sign = 2 * owner_core - 1
        for slot, moved in enumerate(offsets):
            owner_z = lax.rem(z + sign * moved + Z, Z)
            start = ((owner_y * Z + owner_z) * C + owner_core) * rows
            pltpu.make_async_copy(
                piece.at[pl.ds(slot * rows, rows)],
                full.at[pl.ds(pl.multiple_of(start, rows), rows)],
                sem,
            ).start()
    pltpu.make_async_copy(full, full, sem).wait()
    features = full.shape[0]
    chunk = 512
    total = jnp.zeros(projected.shape, jnp.float32)
    for first in range(0, features, chunk):
        cols = slice(first, first + chunk)
        unit = tokens[:, cols].astype(jnp.float32) * inv[...]
        normed = (unit * gain[:, cols].astype(jnp.float32)).astype(jnp.bfloat16)
        total += jnp.dot(normed, full[cols, :], preferred_element_type=jnp.float32)
    projected[...] = total.astype(jnp.bfloat16)
    above = upstream[...]
    inner = jnp.sum(above.astype(jnp.float32) * total, axis=1, keepdims=True) / features
    for first in range(0, features, chunk):
        cols = slice(first, first + chunk)
        grad = lax.dot_general(
            above, full[cols, :], (((1,), (1,)), ((), ())), preferred_element_type=jnp.float32
        )
        unit = tokens[:, cols].astype(jnp.float32) * inv[...]
        gained = grad * gain[:, cols].astype(jnp.float32)
        token_grad[:, cols] = (inv[...] * (gained - unit * inner)).astype(jnp.bfloat16)


def shards(tokens, norm_gain, weight, cotangent, global_params, local_params, momentum, fragment):
    chosen = fragment[0]
    global_row = lax.dynamic_index_in_dim(global_params, chosen, 0, keepdims=False)
    moment_row = lax.dynamic_index_in_dim(momentum, chosen, 0, keepdims=False)
    local_row = lax.dynamic_index_in_dim(local_params[0], chosen, 0, keepdims=False)
    difference = global_row - local_row
    replica_count = lax.axis_size("replica")
    spread = jnp.broadcast_to(difference.reshape(1, -1, 128), (replica_count, difference.size // 128, 128))
    everyone = lax.all_to_all(spread, "replica", 0, 0)
    pseudo = jnp.sum(everyone, axis=0).reshape(-1) / replica_count
    momentum_next = outer_momentum * moment_row + pseudo
    global_next = global_row - outer_rate * (pseudo + outer_momentum * momentum_next)

    own = weight[0]
    rows = own.shape[0]
    held = own
    for hop in HOPS[:-1]:
        held = jnp.concatenate([held, along_z(held, hop)], axis=0)
    last = along_z(held, HOPS[-1])
    held_y = across_y(held)
    last_y = across_y(last)
    mine = [held, held_y, last, last_y]
    other = [across_core(piece) for piece in mine]
    early = [offset(slot, HOPS[:-1]) for slot in range(2 ** (len(HOPS) - 1))]
    late = [moved + HOPS[-1] for moved in early]
    layout = [
        (other_y, other_core, offsets)
        for other_core in (False, True)
        for offsets in (early, late)
        for other_y in (False, True)
    ]
    block = tokens[0]
    floated = block.astype(jnp.float32)
    inv = lax.rsqrt(jnp.mean(floated * floated, axis=1, keepdims=True) + epsilon)
    count, features = block.shape
    width = own.shape[1]
    vmem = pl.BlockSpec(memory_space=pltpu.VMEM)
    projected, token_grad = pl.pallas_call(
        functools.partial(layer_kernel, rows, layout),
        out_shape=(
            jax.ShapeDtypeStruct((count, width), jnp.bfloat16),
            jax.ShapeDtypeStruct((count, features), jnp.bfloat16),
        ),
        in_specs=[pl.BlockSpec(memory_space=pl.ANY)] * len(layout) + [vmem] * 4,
        out_specs=(vmem, vmem),
        scratch_shapes=[pltpu.VMEM((features, width), jnp.bfloat16), pltpu.SemaphoreType.DMA],
        compiler_params=pltpu.CompilerParams(vmem_limit_bytes=24 * 2**20),
        cost_estimate=pl.CostEstimate(flops=4 * count * features * width, bytes_accessed=8 * 2**20, transcendentals=0),
    )(*mine, *other, block, inv, norm_gain, cotangent[0])
    return (projected[None], token_grad[None], global_next, momentum_next)


def solution(mesh):
    placed = (
        P("replica", "fsdp", None),
        P("replica", None),
        P("replica", "fsdp", None),
        P("replica", "fsdp", None),
        P(None, "fsdp"),
        P("replica", None, "fsdp"),
        P(None, "fsdp"),
        P(),
    )
    return jax.shard_map(
        shards,
        mesh=mesh,
        in_specs=placed,
        out_specs=(P("replica", "fsdp", None), P("replica", "fsdp", None), P("fsdp"), P("fsdp")),
        check_vma=False,
    )
```

time: 314 us -> 133 us (0.42)
  waiting for transfers between devices: 258 us -> 12.4 us
  starting transfers between devices: 0.04 us -> 102 us
  blocking collectives: 28.1 us -> 0 us
  between operations: 14.7 us -> 1.53 us
  Pallas kernels: 0 us -> 7.39 us
  matrix products: 5.26 us -> 0 us
    all_gather x1 -> x0, waiting for transfers between devices: 257 us -> none  [shards(): full_weight = lax.all_gather(weight, 'fsdp', axis=1, tiled=True)[0]]
    ppermute x0 -> x11, starting transfers between devices: none -> 97.2 us  [the longest x5 65.2 us: along_z(): lax.ppermute(array, 'fsdp', pairs(lambda y, z, c: (y, z + (hop if c == 0...]
    psum x1 -> x0, blocking collectives: 28.1 us -> none  [shards(): summed = lax.psum(difference, 'replica')]
    ppermute x0 -> x11, waiting for transfers between devices: none -> 12.4 us  [the longest x5 12.3 us: along_z(): lax.ppermute(array, 'fsdp', pairs(lambda y, z, c: (y, z + (hop if c == 0...]
    pallas_call x0 -> x1, Pallas kernels: none -> 7.39 us  [shards(): pl.pallas_call(functools.partial(layer_kernel, rows, layout), out_shape=(...]
    dot_general x2 -> x0, matrix products: 5.26 us -> none  [the longest x1 3.85 us: shards(): lax.dot_general(upstream, full_weight, (((1,), (1,)), ((), ())), preferre...]
    all_to_all x0 -> x1, starting transfers between devices: none -> 5.16 us  [shards(): everyone = lax.all_to_all(spread, 'replica', 0, 0)]
  transfers between devices with their start and end apart: 1 -> 12, of which waited for: 1 -> 4; matrix products, arithmetic and copies ran while one was open for 2% -> 4% of each run, Pallas kernels for 0% -> 0%
where the time goes in v1:
time: 133 us; the launch traced here: 132 us
  starting transfers between devices  102 us (77%)
  waiting for transfers between devices  12.4 us (9%)
  Pallas kernels  7.39 us (6%)
  other arithmetic  5.2 us (4%)
  local copies, waits for them, and re-layouts  2.68 us (2%)
  between operations  1.53 us (1%)
    ppermute x5, starting transfers between devices, along_z(): lax.ppermute(array, 'fsdp', pairs(lambda y, z, c: (y, z + (hop if c == 0...  65.2 us
    ppermute x4, starting transfers between devices, across_core(): return lax.ppermute(array, 'fsdp', pairs(lambda y, z, c: (y, z, 1 - c)))  25.2 us
    ppermute x5, waiting for transfers between devices, along_z(): lax.ppermute(array, 'fsdp', pairs(lambda y, z, c: (y, z + (hop if c == 0...  12.3 us
    pallas_call x1, Pallas kernels, shards(): pl.pallas_call(functools.partial(layer_kernel, rows, layout), out_shape=(...  7.39 us
    ppermute x2, starting transfers between devices, across_y(): return lax.ppermute(array, 'fsdp', pairs(lambda y, z, c: (1 - y, z, c)))  6.78 us
    all_to_all x1, starting transfers between devices, shards(): everyone = lax.all_to_all(spread, 'replica', 0, 0)  5.16 us
  transfers between devices with their start and end apart: 12, of which 4 were waited for; matrix products, arithmetic and copies ran while one was open for 4% of the time, Pallas kernels for 0%

profile of v1, /device:TPU:1, one launch (start us, length us, event | category | flops | bytes accessed | tf_op | source)
XLA Modules:
  0.0 131.6 jit_solution(2252689070030853133)
XLA Ops:
  0.6 0.0 copy-start
  0.6 29.7 %collective-permute-start = (bf16[32,512]{1,0:T(8,128)(2,1)}, bf16[32,512]{1,0:T(8,128)(2,1)S(1)}, u32[]{:S(2)}, u32[]{:S(2)}) collective-permute-start(bf16[32,512]{1,0:T(8,128)(2,1)} %bitcast.27), channel_id=1, source_target_pairs={{0,256},{8,264},{16,272},{24,280},{32,288},{40,296},{48,304},{56,3... | collective-permute-start | bytes 98312 | tf_op jit(solution)/shard_map/ppermute | solution.py:32
  31.0 1.1 collective-permute-done
  32.0 0.8 pad_maximum_fusion.2
  32.8 15.5 %collective-permute-start.1 = (bf16[64,512]{1,0:T(8,128)(2,1)S(1)}, bf16[64,512]{1,0:T(8,128)(2,1)S(1)}, u32[]{:S(2)}, u32[]{:S(2)}) collective-permute-start(bf16[64,512]{1,0:T(8,128)(2,1)S(1)} %pad_maximum_fusion.2), channel_id=1, source_target_pairs={{0,128},{8,392},{16,144},{24,408},{32,160},{40,424},{48,176},{56,4... | collective-permute-start | bytes 196616 | tf_op jit(solution)/shard_map/ppermute | solution.py:32
  48.3 0.0 copy-done
  48.3 1.3 collective-permute-done.1
  49.6 0.8 pad_maximum_fusion.1
  50.4 12.1 %collective-permute-start.2 = (bf16[128,512]{1,0:T(8,128)(2,1)S(1)}, bf16[128,512]{1,0:T(8,128)(2,1)S(1)}, u32[]{:S(2)}, u32[]{:S(2)}) collective-permute-start(bf16[128,512]{1,0:T(8,128)(2,1)S(1)} %pad_maximum_fusion.1), channel_id=1, source_target_pairs={{0,64},{8,456},{16,80},{24,472},{32,96},{40,488},{48,112},{56,504}... | collective-permute-start | bytes 393224 | tf_op jit(solution)/shard_map/ppermute | solution.py:32
  62.5 0.8 constant_dynamic-update-slice_fusion.4
  63.2 4.9 %collective-permute-done.2 = bf16[128,512]{1,0:T(8,128)(2,1)S(1)} collective-permute-done((bf16[128,512]{1,0:T(8,128)(2,1)S(1)}, bf16[128,512]{1,0:T(8,128)(2,1)S(1)}, u32[]{:S(2)}, u32[]{:S(2)}) %collective-permute-start.2) | collective-permute-done | bytes 131104 | tf_op jit(solution)/shard_map/ppermute | solution.py:32
  68.2 0.8 pad_maximum_fusion
  69.0 0.0 copy-start.1
  69.0 6.1 %collective-permute-start.3 = (bf16[256,512]{1,0:T(8,128)(2,1)S(1)}, bf16[256,512]{1,0:T(8,128)(2,1)S(1)}, u32[]{:S(2)}, u32[]{:S(2)}) collective-permute-start(bf16[256,512]{1,0:T(8,128)(2,1)S(1)} %pad_maximum_fusion), channel_id=1, source_target_pairs={{0,32},{8,488},{16,48},{24,504},{32,64},{40,8},{48,80},{56,24},{64... | collective-permute-start | bytes 786440 | tf_op jit(solution)/shard_map/ppermute | solution.py:32
  75.1 5.1 %collective-permute-done.3 = bf16[256,512]{1,0:T(8,128)(2,1)S(1)} collective-permute-done((bf16[256,512]{1,0:T(8,128)(2,1)S(1)}, bf16[256,512]{1,0:T(8,128)(2,1)S(1)}, u32[]{:S(2)}, u32[]{:S(2)}) %collective-permute-start.3) | collective-permute-done | bytes 262176 | tf_op jit(solution)/shard_map/ppermute | solution.py:32
  80.2 1.9 %collective-permute-start.5 = (bf16[512,512]{1,0:T(8,128)(2,1)S(1)}, bf16[512,512]{1,0:T(8,128)(2,1)S(1)}, u32[]{:S(2)}, u32[]{:S(2)}) collective-permute-start(bf16[512,512]{1,0:T(8,128)(2,1)S(1)} %constant_dynamic-update-slice_fusion.refs_0_), channel_id=1, source_target_pairs={{0,16},{8,504},{16,32},{24,8},{32,48},{40,24},{48,64},{56,40},{64,... | collective-permute-start | bytes 1572872 | tf_op jit(solution)/shard_map/ppermute | solution.py:32
  82.1 1.0 constant_dynamic-slice_fusion
  83.1 0.7 broadcast_in_dim.14
  83.8 0.0 copy-start.2
  83.8 0.0 copy-start.3
  83.8 5.2 %all-to-all-start = ((f32[8,64,128]{2,1,0:T(8,128)}), f32[8,64,128]{2,1,0:T(8,128)}, u32[]{:S(2)}, u32[]{:S(2)}) async-start(f32[8,64,128]{2,1,0:T(8,128)} %broadcast_in_dim.14), calls=%async_computation | async-start | bytes 524288 | tf_op jit(solution)/shard_map/all_to_all | solution.py:96
  89.0 4.5 %collective-permute-start.4 = (bf16[512,512]{1,0:T(8,128)(2,1)S(1)}, bf16[512,512]{1,0:T(8,128)(2,1)S(1)}, u32[]{:S(2)}, u32[]{:S(2)}) collective-permute-start(bf16[512,512]{1,0:T(8,128)(2,1)S(1)} %constant_dynamic-update-slice_fusion.refs_0_), channel_id=1, source_target_pairs={{0,512},{8,520},{16,528},{24,536},{32,544},{40,552},{48,560},{56,5... | collective-permute-start | bytes 1572872 | tf_op jit(solution)/shard_map/ppermute | solution.py:36
  93.5 0.0 collective-permute-done.5.refs_2_
  93.5 2.3 %collective-permute-start.6 = (bf16[512,512]{1,0:T(8,128)(2,1)S(1)}, bf16[512,512]{1,0:T(8,128)(2,1)}, u32[]{:S(2)}, u32[]{:S(2)}) collective-permute-start(bf16[512,512]{1,0:T(8,128)(2,1)S(1)} %collective-permute-done.5.refs_2_), channel_id=1, source_target_pairs={{0,512},{8,520},{16,528},{24,536},{32,544},{40,552},{48,560},{56,5... | collective-permute-start | bytes 1572872 | tf_op jit(solution)/shard_map/ppermute | solution.py:36
  95.8 1.0 dynamic-slice_multiply_fusion
  96.8 8.1 %collective-permute-start.7 = (bf16[512,512]{1,0:T(8,128)(2,1)S(1)}, bf16[512,512]{1,0:T(8,128)(2,1)}, u32[]{:S(2)}, u32[]{:S(2)}) collective-permute-start(bf16[512,512]{1,0:T(8,128)(2,1)S(1)} %constant_dynamic-update-slice_fusion.refs_0_), channel_id=1, source_target_pairs={{0,8},{8,0},{16,24},{24,16},{32,40},{40,32},{48,56},{56,48},{64,72... | collective-permute-start | bytes 1572872 | tf_op jit(solution)/shard_map/ppermute | solution.py:40
  104.9 1.9 %collective-permute-start.9 = (bf16[512,512]{1,0:T(8,128)(2,1)S(1)}, bf16[512,512]{1,0:T(8,128)(2,1)}, u32[]{:S(2)}, u32[]{:S(2)}) collective-permute-start(bf16[512,512]{1,0:T(8,128)(2,1)S(1)} %collective-permute-done.5.refs_2_), channel_id=1, source_target_pairs={{0,8},{8,0},{16,24},{24,16},{32,40},{40,32},{48,56},{56,48},{64,72... | collective-permute-start | bytes 1572872 | tf_op jit(solution)/shard_map/ppermute | solution.py:40
  106.9 0.0 collective-permute-done.4.refs_1_
  106.9 8.6 %collective-permute-start.8 = (bf16[512,512]{1,0:T(8,128)(2,1)S(1)}, bf16[512,512]{1,0:T(8,128)(2,1)}, u32[]{:S(2)}, u32[]{:S(2)}) collective-permute-start(bf16[512,512]{1,0:T(8,128)(2,1)S(1)} %collective-permute-done.4.refs_1_), channel_id=1, source_target_pairs={{0,8},{8,0},{16,24},{24,16},{32,40},{40,32},{48,56},{56,48},{64,72... | collective-permute-start | bytes 1572872 | tf_op jit(solution)/shard_map/ppermute | solution.py:40
  115.5 0.0 collective-permute-done.6.refs_3_
  115.5 6.5 %collective-permute-start.10 = (bf16[512,512]{1,0:T(8,128)(2,1)}, bf16[512,512]{1,0:T(8,128)(2,1)}, u32[]{:S(2)}, u32[]{:S(2)}) collective-permute-start(bf16[512,512]{1,0:T(8,128)(2,1)} %collective-permute-done.6.refs_3_), channel_id=1, source_target_pairs={{0,8},{8,0},{16,24},{24,16},{32,40},{40,32},{48,56},{56,48},{64,72... | collective-permute-start | bytes 1572872 | tf_op jit(solution)/shard_map/ppermute | solution.py:40
  122.1 0.0 copy-done.1
  122.1 0.3 multiply_reduce_fusion
  122.4 0.1 copy.13.refs_9_
  122.5 0.0 all-to-all-done
  122.5 1.0 reduce_sum.19
  123.5 0.6 fusion.1
  124.1 0.0 collective-permute-done.7.refs_4_
  124.1 0.0 collective-permute-done.8.refs_5_
  124.1 0.0 collective-permute-done.9.refs_6_
  124.1 0.0 collective-permute-done.10.refs_7_
  124.2 0.0 copy-done.2
  124.2 0.0 copy-done.3
  124.2 7.4 %shard_map.111 = (bf16[128,512]{1,0:T(8,128)(2,1)}, bf16[128,4096]{1,0:T(8,128)(2,1)}) custom-call(bf16[512,512]{1,0:T(8,128)(2,1)S(1)} %constant_dynamic-update-slice_fusion.refs_0_, bf16[512,512]{1,0:T(8,128)(2,1)S(1)} %collective-permute-done.4.refs_1_, bf16[512,512]{1,0:T(8,128)(2,1)S(1)} %collective-permute-done.5.refs_2_, ...), custom_call_target="tpu_custom_call" | custom-call | flops 1073741824 | bytes 8388608 | tf_op jit(solution)/shard_map/pallas_call | solution.py:125
  (7 shorter events, 0.1 us)
Async XLA Ops:
  0.6 47.7 %copy-start = (f32[16,8192]{1,0:T(8,128)S(1)}, f32[16,8192]{1,0:T(8,128)}, u32[]{:S(2)}) copy-start(f32[16,8192]{1,0:T(8,128)} %param.12) | copy-start | bytes 1572868
  0.6 31.4 %collective-permute-start = (bf16[32,512]{1,0:T(8,128)(2,1)}, bf16[32,512]{1,0:T(8,128)(2,1)S(1)}, u32[]{:S(2)}, u32[]{:S(2)}) collective-permute-start(bf16[32,512]{1,0:T(8,128)(2,1)} %bitcast.27), channel_id=1, source_target_pairs={{0,256},{8,264},{16,272},{24,280},{32,288},{40,296},{48,304},{56,3... | collective-permute-start | bytes 98312 | tf_op jit(solution)/shard_map/ppermute | solution.py:32
  32.8 16.8 %collective-permute-start.1 = (bf16[64,512]{1,0:T(8,128)(2,1)S(1)}, bf16[64,512]{1,0:T(8,128)(2,1)S(1)}, u32[]{:S(2)}, u32[]{:S(2)}) collective-permute-start(bf16[64,512]{1,0:T(8,128)(2,1)S(1)} %pad_maximum_fusion.2), channel_id=1, source_target_pairs={{0,128},{8,392},{16,144},{24,408},{32,160},{40,424},{48,176},{56,4... | collective-permute-start | bytes 196616 | tf_op jit(solution)/shard_map/ppermute | solution.py:32
  50.4 17.8 %collective-permute-start.2 = (bf16[128,512]{1,0:T(8,128)(2,1)S(1)}, bf16[128,512]{1,0:T(8,128)(2,1)S(1)}, u32[]{:S(2)}, u32[]{:S(2)}) collective-permute-start(bf16[128,512]{1,0:T(8,128)(2,1)S(1)} %pad_maximum_fusion.1), channel_id=1, source_target_pairs={{0,64},{8,456},{16,80},{24,472},{32,96},{40,488},{48,112},{56,504}... | collective-permute-start | bytes 393224 | tf_op jit(solution)/shard_map/ppermute | solution.py:32
  69.0 53.1 %copy-start.1 = (bf16[1,128,4096]{2,1,0:T(8,128)(2,1)S(1)}, bf16[1,128,4096]{2,1,0:T(8,128)(2,1)}, u32[]{:S(2)}) copy-start(bf16[1,128,4096]{2,1,0:T(8,128)(2,1)} %param.8) | copy-start | bytes 3145732
  69.0 11.2 %collective-permute-start.3 = (bf16[256,512]{1,0:T(8,128)(2,1)S(1)}, bf16[256,512]{1,0:T(8,128)(2,1)S(1)}, u32[]{:S(2)}, u32[]{:S(2)}) collective-permute-start(bf16[256,512]{1,0:T(8,128)(2,1)S(1)} %pad_maximum_fusion), channel_id=1, source_target_pairs={{0,32},{8,488},{16,48},{24,504},{32,64},{40,8},{48,80},{56,24},{64... | collective-permute-start | bytes 786440 | tf_op jit(solution)/shard_map/ppermute | solution.py:32
  80.2 13.3 %collective-permute-start.5 = (bf16[512,512]{1,0:T(8,128)(2,1)S(1)}, bf16[512,512]{1,0:T(8,128)(2,1)S(1)}, u32[]{:S(2)}, u32[]{:S(2)}) collective-permute-start(bf16[512,512]{1,0:T(8,128)(2,1)S(1)} %constant_dynamic-update-slice_fusion.refs_0_), channel_id=1, source_target_pairs={{0,16},{8,504},{16,32},{24,8},{32,48},{40,24},{48,64},{56,40},{64,... | collective-permute-start | bytes 1572872 | tf_op jit(solution)/shard_map/ppermute | solution.py:32
  83.8 40.3 %copy-start.2 = (bf16[1,128,512]{2,1,0:T(8,128)(2,1)S(1)}, bf16[1,128,512]{2,1,0:T(8,128)(2,1)}, u32[]{:S(2)}) copy-start(bf16[1,128,512]{2,1,0:T(8,128)(2,1)} %param.11) | copy-start | bytes 393220
  83.8 40.3 %copy-start.3 = (bf16[1,4096]{1,0:T(2,128)(2,1)S(1)}, bf16[1,4096]{1,0:T(2,128)(2,1)}, u32[]{:S(2)}) copy-start(bf16[1,4096]{1,0:T(2,128)(2,1)} %refs_10_.1) | copy-start | bytes 24580
  83.8 38.7 %all-to-all-start = ((f32[8,64,128]{2,1,0:T(8,128)}), f32[8,64,128]{2,1,0:T(8,128)}, u32[]{:S(2)}, u32[]{:S(2)}) async-start(f32[8,64,128]{2,1,0:T(8,128)} %broadcast_in_dim.14), calls=%async_computation | async-start | bytes 524288 | tf_op jit(solution)/shard_map/all_to_all | solution.py:96
  89.0 17.9 %collective-permute-start.4 = (bf16[512,512]{1,0:T(8,128)(2,1)S(1)}, bf16[512,512]{1,0:T(8,128)(2,1)S(1)}, u32[]{:S(2)}, u32[]{:S(2)}) collective-permute-start(bf16[512,512]{1,0:T(8,128)(2,1)S(1)} %constant_dynamic-update-slice_fusion.refs_0_), channel_id=1, source_target_pairs={{0,512},{8,520},{16,528},{24,536},{32,544},{40,552},{48,560},{56,5... | collective-permute-start | bytes 1572872 | tf_op jit(solution)/shard_map/ppermute | solution.py:36
  93.5 22.0 %collective-permute-start.6 = (bf16[512,512]{1,0:T(8,128)(2,1)S(1)}, bf16[512,512]{1,0:T(8,128)(2,1)}, u32[]{:S(2)}, u32[]{:S(2)}) collective-permute-start(bf16[512,512]{1,0:T(8,128)(2,1)S(1)} %collective-permute-done.5.refs_2_), channel_id=1, source_target_pairs={{0,512},{8,520},{16,528},{24,536},{32,544},{40,552},{48,560},{56,5... | collective-permute-start | bytes 1572872 | tf_op jit(solution)/shard_map/ppermute | solution.py:36
  96.8 27.3 %collective-permute-start.7 = (bf16[512,512]{1,0:T(8,128)(2,1)S(1)}, bf16[512,512]{1,0:T(8,128)(2,1)}, u32[]{:S(2)}, u32[]{:S(2)}) collective-permute-start(bf16[512,512]{1,0:T(8,128)(2,1)S(1)} %constant_dynamic-update-slice_fusion.refs_0_), channel_id=1, source_target_pairs={{0,8},{8,0},{16,24},{24,16},{32,40},{40,32},{48,56},{56,48},{64,72... | collective-permute-start | bytes 1572872 | tf_op jit(solution)/shard_map/ppermute | solution.py:40
  104.9 19.2 %collective-permute-start.9 = (bf16[512,512]{1,0:T(8,128)(2,1)S(1)}, bf16[512,512]{1,0:T(8,128)(2,1)}, u32[]{:S(2)}, u32[]{:S(2)}) collective-permute-start(bf16[512,512]{1,0:T(8,128)(2,1)S(1)} %collective-permute-done.5.refs_2_), channel_id=1, source_target_pairs={{0,8},{8,0},{16,24},{24,16},{32,40},{40,32},{48,56},{56,48},{64,72... | collective-permute-start | bytes 1572872 | tf_op jit(solution)/shard_map/ppermute | solution.py:40
  106.9 17.2 %collective-permute-start.8 = (bf16[512,512]{1,0:T(8,128)(2,1)S(1)}, bf16[512,512]{1,0:T(8,128)(2,1)}, u32[]{:S(2)}, u32[]{:S(2)}) collective-permute-start(bf16[512,512]{1,0:T(8,128)(2,1)S(1)} %collective-permute-done.4.refs_1_), channel_id=1, source_target_pairs={{0,8},{8,0},{16,24},{24,16},{32,40},{40,32},{48,56},{56,48},{64,72... | collective-permute-start | bytes 1572872 | tf_op jit(solution)/shard_map/ppermute | solution.py:40
  115.5 8.6 %collective-permute-start.10 = (bf16[512,512]{1,0:T(8,128)(2,1)}, bf16[512,512]{1,0:T(8,128)(2,1)}, u32[]{:S(2)}, u32[]{:S(2)}) collective-permute-start(bf16[512,512]{1,0:T(8,128)(2,1)} %collective-permute-done.6.refs_3_), channel_id=1, source_target_pairs={{0,8},{8,0},{16,24},{24,16},{32,40},{40,32},{48,56},{56,48},{64,72... | collective-permute-start | bytes 1572872 | tf_op jit(solution)/shard_map/ppermute | solution.py:40

commit v2 on v1

v2 whole, which is shorter than its diff:
```python
import functools

import jax
import jax.numpy as jnp
from jax import lax
from jax.experimental import pallas as pl
from jax.experimental.pallas import tpu as pltpu
from jax.sharding import PartitionSpec as P

epsilon = 1e-05
outer_momentum = 0.9
outer_rate = 0.7

Y, Z, C = 2, 32, 2
VMEM = pl.BlockSpec(memory_space=pltpu.VMEM)
SMEM = pl.BlockSpec(memory_space=pltpu.SMEM)
ANY = pl.BlockSpec(memory_space=pl.ANY)


def at(y, z, c):
    return (y * Z + z % Z) * C + c


def sources():
    return [(y, z, c) for y in range(Y) for z in range(Z) for c in range(C)]


def send(array, step):
    return lax.ppermute(array, "fsdp", [(at(*here), at(*step(*here))) for here in sources()])


def along_z(array, hop):
    return send(array, lambda y, z, c: (y, z + (hop if c == 0 else -hop), c))


def across_y(array):
    return send(array, lambda y, z, c: (1 - y, z, c))


def across_core(array):
    return send(array, lambda y, z, c: (y, z, 1 - c))


def chip_kernel(own, first, second, out):
    rows = own.shape[0]
    core = lax.rem(lax.axis_index("fsdp"), C)

    @pl.when(core == 0)
    def _():
        out[:rows, :] = own[...]
        out[rows:, :] = first[...]

    @pl.when(core != 0)
    def _():
        out[:rows, :] = first[...]
        out[rows:, :] = second[...]


def chip_rows(own):
    first = send(own, lambda y, z, c: (y, z - 1, 1) if c == 0 else (y, z, 0))
    down = [(at(y, z, c), at(y, z - 1, c)) for y, z, c in sources() if c == 1]
    second = lax.ppermute(own, "fsdp", down)
    rows, width = own.shape
    return pl.pallas_call(
        chip_kernel,
        out_shape=jax.ShapeDtypeStruct((C * rows, width), own.dtype),
        in_specs=[VMEM] * 3,
        out_specs=VMEM,
        compiler_params=pltpu.CompilerParams(vmem_limit_bytes=2**20),
    )(own, first, second)


def join_kernel(first, second, *refs):
    out, rows = refs[-1], first.shape[0]
    out[:rows, :] = first[...]
    out[rows:, :] = second[...]


def join(first, second, *ahead, flops=0):
    rows, width = first.shape
    return pl.pallas_call(
        join_kernel,
        out_shape=jax.ShapeDtypeStruct((2 * rows, width), first.dtype),
        in_specs=[VMEM] * 2 + [ANY] * len(ahead),
        out_specs=VMEM,
        compiler_params=pltpu.CompilerParams(vmem_limit_bytes=4 * 2**20),
        cost_estimate=pl.CostEstimate(flops=flops, bytes_accessed=4 * rows * width, transcendentals=0),
    )(first, second, *ahead)


def pick_kernel(chosen, params, local, momentum, ahead, spread, params_row, moment_row, held, sems):
    index = chosen[0]
    group = pl.multiple_of(lax.div(index, 8) * 8, 8)
    row = lax.rem(index, 8)
    copies = [
        pltpu.make_async_copy(source.at[pl.ds(group, 8)], held.at[slot], sems.at[slot])
        for slot, source in enumerate((params, local, momentum))
    ]
    for copy in copies:
        copy.start()
    for copy in copies:
        copy.wait()
    wanted = lax.broadcasted_iota(jnp.int32, (8, 128), 0) == row

    def taken(slot, lanes):
        return jnp.sum(jnp.where(wanted, held[slot, :, lanes], 0.0), axis=0, keepdims=True)

    for line in range(params_row.shape[0]):
        lanes = slice(128 * line, 128 * line + 128)
        mine = taken(0, lanes)
        spread[:, line, :] = jnp.broadcast_to(mine - taken(1, lanes), (spread.shape[0], 128))
        params_row[line : line + 1, :] = mine
        moment_row[line : line + 1, :] = taken(2, lanes)


def pick(fragment, params, local, momentum, replicas, ahead):
    length = params.shape[1]
    lines = length // 128
    row = jax.ShapeDtypeStruct((lines, 128), jnp.float32)
    return pl.pallas_call(
        pick_kernel,
        out_shape=(jax.ShapeDtypeStruct((replicas, lines, 128), jnp.float32), row, row),
        in_specs=[SMEM] + [ANY] * 4,
        out_specs=(VMEM,) * 3,
        scratch_shapes=[pltpu.VMEM((3, 8, length), jnp.float32), pltpu.SemaphoreType.DMA((3,))],
        compiler_params=pltpu.CompilerParams(vmem_limit_bytes=4 * 2**20),
    )(fragment, params, local, momentum, ahead)


def side_kernel(everyone, params_row, moment_row, tokens, params_next, moment_next, inv):
    count = everyone.shape[0]
    total = everyone[0]
    for replica in range(1, count):
        total = total + everyone[replica]
    pseudo = total / count
    moment = outer_momentum * moment_row[...] + pseudo
    moment_next[...] = moment
    params_next[...] = params_row[...] - outer_rate * (pseudo + outer_momentum * moment)
    features = tokens.shape[1]
    squares = jnp.zeros(inv.shape, jnp.float32)
    for first in range(0, features, 512):
        floated = tokens[:, first : first + 512].astype(jnp.float32)
        squares = squares + jnp.sum(floated * floated, axis=1, keepdims=True)
    inv[...] = lax.rsqrt(squares / features + epsilon)


def side(everyone, params_row, moment_row, tokens):
    row = jax.ShapeDtypeStruct(params_row.shape, jnp.float32)
    return pl.pallas_call(
        side_kernel,
        out_shape=(row, row, jax.ShapeDtypeStruct((tokens.shape[0], 1), jnp.float32)),
        in_specs=[VMEM] * 4,
        out_specs=(VMEM,) * 3,
        compiler_params=pltpu.CompilerParams(vmem_limit_bytes=4 * 2**20),
    )(everyone, params_row, moment_row, tokens)


def layer_kernel(rows, layout, *refs):
    pieces = refs[: len(layout)]
    tokens, inv, gain, cotangent, projected, token_grad, full, staged, upstream, sems = refs[len(layout) :]
    fetch = pltpu.make_async_copy(cotangent, upstream, sems.at[len(layout)])
    fetch.start()
    loads, first = [], 0
    for number, piece in enumerate(pieces):
        target = staged.at[pl.ds(first, piece.shape[0])]
        loads.append((first, pltpu.make_async_copy(piece, target, sems.at[number])))
        loads[-1][1].start()
        first += piece.shape[0]
    place = lax.axis_index("fsdp")
    core = lax.rem(place, C)
    chip = lax.div(place, C)
    z, y = lax.rem(chip, Z), lax.div(chip, Z)
    for (first, load), (other_y, other_core, offsets) in zip(loads, layout):
        owner_y = 1 - y if other_y else y
        owner_core = 1 - core if other_core else core
        load.wait()
        for slot, moved in enumerate(offsets):
            owner_z = lax.rem(z + Z + jnp.where(owner_core == 0, -moved, moved + 1), Z)
            start = pl.multiple_of((owner_y * Z + owner_z) * rows, rows)
            full[pl.ds(start, rows), :] = staged[first + slot * rows : first + (slot + 1) * rows, :]
    features = full.shape[0]
    chunk = 512
    total = jnp.zeros(projected.shape, jnp.float32)
    for first in range(0, features, chunk):
        cols = slice(first, first + chunk)
        unit = tokens[:, cols].astype(jnp.float32) * inv[...]
        normed = (unit * gain[:, cols].astype(jnp.float32)).astype(jnp.bfloat16)
        total += jnp.dot(normed, full[cols, :], preferred_element_type=jnp.float32)
    projected[...] = total.astype(jnp.bfloat16)
    fetch.wait()
    above = upstream[...]
    inner = jnp.sum(above.astype(jnp.float32) * total, axis=1, keepdims=True) / features
    for first in range(0, features, chunk):
        cols = slice(first, first + chunk)
        grad = lax.dot_general(
            above, full[cols, :], (((1,), (1,)), ((), ())), preferred_element_type=jnp.float32
        )
        unit = tokens[:, cols].astype(jnp.float32) * inv[...]
        gained = grad * gain[:, cols].astype(jnp.float32)
        token_grad[:, cols] = (inv[...] * (gained - unit * inner)).astype(jnp.bfloat16)


def shards(tokens, norm_gain, weight, cotangent, global_params, local_params, momentum, fragment):
    own = weight[0]
    rows = C * own.shape[0]
    block = tokens[0]
    one = chip_rows(own)
    spread, params_row, moment_row = pick(
        fragment, global_params, local_params[0], momentum, lax.axis_size("replica"), one
    )
    next_one = along_z(one, 8)
    everyone = lax.all_to_all(spread, "replica", 0, 0)
    two = join(one, next_one, flops=10**10)
    next_two = along_z(two, 4)
    global_next, momentum_next, inv = side(everyone, params_row, moment_row, block)
    four = join(two, next_two, inv)
    next_four = along_z(four, 2)
    four_y = across_y(four)
    eight = join(four, next_four, flops=10**10)
    next_four_y = across_y(next_four)
    last = along_z(eight, 1)
    eight_c = across_core(eight)
    eight_y = join(four_y, next_four_y)
    last_y = along_z(eight_y, 1)
    before = (0, 8, 4, 12, 2, 10, 6, 14)
    after = tuple(moved + 1 for moved in before)
    gathered = [
        (eight, False, False, before),
        (eight_c, False, True, before),
        (eight_y, True, False, before),
        (last, False, False, after),
        (across_core(eight_y), True, True, before),
        (across_core(last), False, True, after),
        (last_y, True, False, after),
        (across_core(last_y), True, True, after),
    ]
    layout = [entry[1:] for entry in gathered]
    count, features = block.shape
    width = own.shape[1]
    projected, token_grad = pl.pallas_call(
        functools.partial(layer_kernel, rows, layout),
        out_shape=(
            jax.ShapeDtypeStruct((count, width), jnp.bfloat16),
            jax.ShapeDtypeStruct((count, features), jnp.bfloat16),
        ),
        in_specs=[ANY] * len(layout) + [VMEM] * 3 + [ANY],
        out_specs=(VMEM, VMEM),
        scratch_shapes=[
            pltpu.VMEM((features, width), jnp.bfloat16),
            pltpu.VMEM((features, width), jnp.bfloat16),
            pltpu.VMEM((count, width), jnp.bfloat16),
            pltpu.SemaphoreType.DMA((len(layout) + 1,)),
        ],
        compiler_params=pltpu.CompilerParams(vmem_limit_bytes=16 * 2**20),
        cost_estimate=pl.CostEstimate(flops=4 * count * features * width, bytes_accessed=8 * 2**20, transcendentals=0),
    )(*[entry[0] for entry in gathered], block, inv, norm_gain, cotangent[0])
    return (projected[None], token_grad[None], global_next.reshape(-1), momentum_next.reshape(-1))


def solution(mesh):
    placed = (
        P("replica", "fsdp", None),
        P("replica", None),
        P("replica", "fsdp", None),
        P("replica", "fsdp", None),
        P(None, "fsdp"),
        P("replica", None, "fsdp"),
        P(None, "fsdp"),
        P(),
    )
    return jax.shard_map(
        shards,
        mesh=mesh,
        in_specs=placed,
        out_specs=(P("replica", "fsdp", None), P("replica", "fsdp", None), P("fsdp"), P("fsdp")),
        check_vma=False,
    )
```

time: 133 us -> 98.6 us (0.74)
  starting transfers between devices: 102 us -> 68 us
  waiting for transfers between devices: 12.4 us -> 18.3 us
  other arithmetic: 5.2 us -> 0 us
    ppermute x11 -> x13, starting transfers between devices: 97.2 us -> 63 us  [the longest x12 43.8 us: send(): lax.ppermute(array, 'fsdp', [(at(*here), at(*step(*here))) for here in so...]
    ppermute x11 -> x13, waiting for transfers between devices: 12.4 us -> 17.5 us  [the longest x12 16.2 us: send(): lax.ppermute(array, 'fsdp', [(at(*here), at(*step(*here))) for here in so...]
    pallas_call x1, Pallas kernels: 7.39 us -> 4.13 us  [shards(): pl.pallas_call(functools.partial(layer_kernel, rows, layout), out_shape=(...]
    unnamed x12 -> x14, local copies, waits for them, and re-layouts: 0.81 us -> 3.89 us
    concatenate x3 -> x0, other arithmetic: 2.3 us -> none  [shards(): held = jnp.concatenate([held, along_z(held, hop)], axis=0)]
    pallas_call x0 -> x7, Pallas kernels: none -> 2 us  [the longest x1 1.05 us: pick(): pl.pallas_call(pick_kernel, out_shape=(jax.ShapeDtypeStruct((replicas, li...]
  transfers between devices with their start and end apart: 12 -> 14, of which waited for: 4 -> 7; matrix products, arithmetic and copies ran while one was open for 4% -> 0% of each run, Pallas kernels for 0% -> 2%
where the time goes in v2:
time: 98.6 us; the launch traced here: 97.8 us
  starting transfers between devices  68 us (69%)
  waiting for transfers between devices  18.3 us (19%)
  Pallas kernels  6.12 us (6%)
  local copies, waits for them, and re-layouts  3.89 us (4%)
  between operations  1.5 us (2%)
    ppermute x12, starting transfers between devices, send(): lax.ppermute(array, 'fsdp', [(at(*here), at(*step(*here))) for here in so...  43.8 us
    ppermute x1, starting transfers between devices, chip_rows(): second = lax.ppermute(own, 'fsdp', down)  19.2 us
    ppermute x12, waiting for transfers between devices, send(): lax.ppermute(array, 'fsdp', [(at(*here), at(*step(*here))) for here in so...  16.2 us
    all_to_all x1, starting transfers between devices, shards(): everyone = lax.all_to_all(spread, 'replica', 0, 0)  5.04 us
    pallas_call x1, Pallas kernels, shards(): pl.pallas_call(functools.partial(layer_kernel, rows, layout), out_shape=(...  4.13 us
    unnamed x14, local copies, waits for them, and re-layouts  3.89 us
  transfers between devices with their start and end apart: 14, of which 7 were waited for; matrix products, arithmetic and copies ran while one was open for 0% of the time, Pallas kernels for 2%

profile of v2, /device:TPU:1, one launch (start us, length us, event | category | flops | bytes accessed | tf_op | source)
XLA Modules:
  0.0 97.8 jit_solution(7846086080715287093)
XLA Ops:
  0.6 19.2 %collective-permute-start.1 = (bf16[32,512]{1,0:T(8,128)(2,1)}, bf16[32,512]{1,0:T(8,128)(2,1)S(1)}, u32[]{:S(2)}, u32[]{:S(2)}) collective-permute-start(bf16[32,512]{1,0:T(8,128)(2,1)} %bitcast.12), channel_id=1, source_target_pairs={{8,504},{24,8},{40,24},{56,40},{72,56},{88,72},{104,88},{120,104},... | collective-permute-start | bytes 98312 | tf_op jit(solution)/shard_map/ppermute | solution.py:62
  19.9 0.0 collective-permute-start
  19.9 1.3 %collective-permute-done.1.second = bf16[32,512]{1,0:T(8,128)(2,1)S(1)} collective-permute-done((bf16[32,512]{1,0:T(8,128)(2,1)}, bf16[32,512]{1,0:T(8,128)(2,1)S(1)}, u32[]{:S(2)}, u32[]{:S(2)}) %collective-permute-start.1) | collective-permute-done | bytes 32800 | tf_op jit(solution)/shard_map/ppermute | solution.py:62
  21.2 2.2 %collective-permute-done.first = bf16[32,512]{1,0:T(8,128)(2,1)S(1)} collective-permute-done((bf16[32,512]{1,0:T(8,128)(2,1)}, bf16[32,512]{1,0:T(8,128)(2,1)S(1)}, u32[]{:S(2)}, u32[]{:S(2)}) %collective-permute-start) | collective-permute-done | bytes 32800 | tf_op jit(solution)/shard_map/ppermute | solution.py:29
  23.4 0.0 copy-start.5
  23.4 0.8 copy-done.5
  24.2 8.2 %collective-permute-start.2 = (bf16[64,512]{1,0:T(8,128)(2,1)S(1)}, bf16[64,512]{1,0:T(8,128)(2,1)S(1)}, u32[]{:S(2)}, u32[]{:S(2)}) collective-permute-start(bf16[64,512]{1,0:T(8,128)(2,1)S(1)} %shard_map.111.first.ahead), channel_id=1, source_target_pairs={{0,128},{8,392},{16,144},{24,408},{32,160},{40,424},{48,176},{56,4... | collective-permute-start | bytes 196616 | tf_op jit(solution)/shard_map/ppermute | solution.py:29
  33.0 0.0 copy-start.1
  33.0 1.0 %copy-done.1 = f32[16,8192]{1,0:T(8,128)S(1)} copy-done((f32[16,8192]{1,0:T(8,128)S(1)}, f32[16,8192]{1,0:T(8,128)}, u32[]{:S(2)}) %copy-start.1) | copy-done | bytes 524312
  34.0 0.0 copy-start.2
  34.0 1.0 %copy-done.2 = f32[1,16,8192]{2,1,0:T(8,128)S(1)} copy-done((f32[1,16,8192]{2,1,0:T(8,128)S(1)}, f32[1,16,8192]{2,1,0:T(8,128)}, u32[]{:S(2)}) %copy-start.2) | copy-done | bytes 524312
  35.1 0.0 copy-start.3
  35.1 1.0 %copy-done.3 = f32[16,8192]{1,0:T(8,128)S(1)} copy-done((f32[16,8192]{1,0:T(8,128)S(1)}, f32[16,8192]{1,0:T(8,128)}, u32[]{:S(2)}) %copy-start.3) | copy-done | bytes 524312
  36.1 1.1 %shard_map.113 = (f32[8,64,128]{2,1,0:T(8,128)}, f32[64,128]{1,0:T(8,128)S(1)}, f32[64,128]{1,0:T(8,128)S(1)}) custom-call(s32[1]{0:T(128)S(6)} %copy.12.chosen, f32[16,8192]{1,0:T(8,128)S(1)} %copy-done.1, f32[16,8192]{1,0:T(8,128)S(1)} %bitcast.10, f32[16,8192]{1,0:T(8,128)S(1)} %copy-done.3, bf16[64,512]{1,0:T(8,128)(2,1)S(1)} %shard_map.111.first.ahead), custom_call_target="tpu_custom_call" | custom-call | tf_op jit(solution)/shard_map/pallas_call | solution.py:120
  37.2 5.0 %all-to-all-start = ((f32[8,64,128]{2,1,0:T(8,128)}), f32[8,64,128]{2,1,0:T(8,128)S(1)}, u32[]{:S(2)}, u32[]{:S(2)}) async-start(f32[8,64,128]{2,1,0:T(8,128)} %get-tuple-element.12), calls=%async_computation | async-start | bytes 524288 | tf_op jit(solution)/shard_map/all_to_all | solution.py:212
  42.2 0.0 copy-start
  42.2 0.0 collective-permute-done.2.second
  42.3 5.3 %collective-permute-start.3 = (bf16[128,512]{1,0:T(8,128)(2,1)S(1)}, bf16[128,512]{1,0:T(8,128)(2,1)S(1)}, u32[]{:S(2)}, u32[]{:S(2)}) collective-permute-start(bf16[128,512]{1,0:T(8,128)(2,1)S(1)} %shard_map.112.first), channel_id=1, source_target_pairs={{0,64},{8,456},{16,80},{24,472},{32,96},{40,488},{48,112},{56,504}... | collective-permute-start | bytes 393224 | tf_op jit(solution)/shard_map/ppermute | solution.py:29
  47.6 0.8 all-to-all-done.everyone
  48.4 0.0 copy-done
  48.4 0.8 shard_map.114
  49.2 5.5 %collective-permute-done.3.second = bf16[128,512]{1,0:T(8,128)(2,1)S(1)} collective-permute-done((bf16[128,512]{1,0:T(8,128)(2,1)S(1)}, bf16[128,512]{1,0:T(8,128)(2,1)S(1)}, u32[]{:S(2)}, u32[]{:S(2)}) %collective-permute-start.3) | collective-permute-done | bytes 131104 | tf_op jit(solution)/shard_map/ppermute | solution.py:29
  54.8 1.9 %collective-permute-start.4 = (bf16[256,512]{1,0:T(8,128)(2,1)S(1)}, bf16[256,512]{1,0:T(8,128)(2,1)S(1)}, u32[]{:S(2)}, u32[]{:S(2)}) collective-permute-start(bf16[256,512]{1,0:T(8,128)(2,1)S(1)} %shard_map.115.first), channel_id=1, source_target_pairs={{0,32},{8,488},{16,48},{24,504},{32,64},{40,8},{48,80},{56,24},{64... | collective-permute-start | bytes 786440 | tf_op jit(solution)/shard_map/ppermute | solution.py:29
  56.7 4.5 %collective-permute-start.6 = (bf16[256,512]{1,0:T(8,128)(2,1)S(1)}, bf16[256,512]{1,0:T(8,128)(2,1)S(1)}, u32[]{:S(2)}, u32[]{:S(2)}) collective-permute-start(bf16[256,512]{1,0:T(8,128)(2,1)S(1)} %shard_map.115.first), channel_id=1, source_target_pairs={{0,512},{8,520},{16,528},{24,536},{32,544},{40,552},{48,560},{56,5... | collective-permute-start | bytes 786440 | tf_op jit(solution)/shard_map/ppermute | solution.py:29
  61.2 4.6 %collective-permute-done.4.second = bf16[256,512]{1,0:T(8,128)(2,1)S(1)} collective-permute-done((bf16[256,512]{1,0:T(8,128)(2,1)S(1)}, bf16[256,512]{1,0:T(8,128)(2,1)S(1)}, u32[]{:S(2)}, u32[]{:S(2)}) %collective-permute-start.4) | collective-permute-done | bytes 262176 | tf_op jit(solution)/shard_map/ppermute | solution.py:29
  65.9 4.5 %collective-permute-start.7 = (bf16[256,512]{1,0:T(8,128)(2,1)S(1)}, bf16[256,512]{1,0:T(8,128)(2,1)S(1)}, u32[]{:S(2)}, u32[]{:S(2)}) collective-permute-start(bf16[256,512]{1,0:T(8,128)(2,1)S(1)} %collective-permute-done.4.second), channel_id=1, source_target_pairs={{0,512},{8,520},{16,528},{24,536},{32,544},{40,552},{48,560},{56,5... | collective-permute-start | bytes 786440 | tf_op jit(solution)/shard_map/ppermute | solution.py:29
  70.4 0.0 copy-start.4
  70.4 0.0 copy-start.6
  70.4 3.4 %collective-permute-start.8 = (bf16[512,512]{1,0:T(8,128)(2,1)S(1)}, bf16[512,512]{1,0:T(8,128)(2,1)S(1)}, u32[]{:S(2)}, u32[]{:S(2)}) collective-permute-start(bf16[512,512]{1,0:T(8,128)(2,1)S(1)} %shard_map.116.refs_0_), channel_id=1, source_target_pairs={{0,16},{8,504},{16,32},{24,8},{32,48},{40,24},{48,64},{56,40},{64,... | collective-permute-start | bytes 1572872 | tf_op jit(solution)/shard_map/ppermute | solution.py:29
  73.9 0.0 collective-permute-done.6.first
  73.9 2.3 %collective-permute-done.7.second = bf16[256,512]{1,0:T(8,128)(2,1)S(1)} collective-permute-done((bf16[256,512]{1,0:T(8,128)(2,1)S(1)}, bf16[256,512]{1,0:T(8,128)(2,1)S(1)}, u32[]{:S(2)}, u32[]{:S(2)}) %collective-permute-start.7) | collective-permute-done | bytes 262176 | tf_op jit(solution)/shard_map/ppermute | solution.py:29
  76.3 4.4 %collective-permute-start.11 = (bf16[512,512]{1,0:T(8,128)(2,1)S(1)}, bf16[512,512]{1,0:T(8,128)(2,1)S(1)}, u32[]{:S(2)}, u32[]{:S(2)}) collective-permute-start(bf16[512,512]{1,0:T(8,128)(2,1)S(1)} %shard_map.117.refs_2_), channel_id=1, source_target_pairs={{0,16},{8,504},{16,32},{24,8},{32,48},{40,24},{48,64},{56,40},{64,... | collective-permute-start | bytes 1572872 | tf_op jit(solution)/shard_map/ppermute | solution.py:29
  80.7 1.9 %collective-permute-start.5 = (bf16[512,512]{1,0:T(8,128)(2,1)S(1)}, bf16[512,512]{1,0:T(8,128)(2,1)S(1)}, u32[]{:S(2)}, u32[]{:S(2)}) collective-permute-start(bf16[512,512]{1,0:T(8,128)(2,1)S(1)} %shard_map.116.refs_0_), channel_id=1, source_target_pairs={{0,8},{8,0},{16,24},{24,16},{32,40},{40,32},{48,56},{56,48},{64,72... | collective-permute-start | bytes 1572872 | tf_op jit(solution)/shard_map/ppermute | solution.py:29
  82.6 2.4 %collective-permute-start.9 = (bf16[512,512]{1,0:T(8,128)(2,1)S(1)}, bf16[512,512]{1,0:T(8,128)(2,1)S(1)}, u32[]{:S(2)}, u32[]{:S(2)}) collective-permute-start(bf16[512,512]{1,0:T(8,128)(2,1)S(1)} %shard_map.117.refs_2_), channel_id=1, source_target_pairs={{0,8},{8,0},{16,24},{24,16},{32,40},{40,32},{48,56},{56,48},{64,72... | collective-permute-start | bytes 1572872 | tf_op jit(solution)/shard_map/ppermute | solution.py:29
  85.0 0.0 collective-permute-done.8.refs_3_
  85.0 1.9 %collective-permute-start.10 = (bf16[512,512]{1,0:T(8,128)(2,1)S(1)}, bf16[512,512]{1,0:T(8,128)(2,1)S(1)}, u32[]{:S(2)}, u32[]{:S(2)}) collective-permute-start(bf16[512,512]{1,0:T(8,128)(2,1)S(1)} %collective-permute-done.8.refs_3_), channel_id=1, source_target_pairs={{0,8},{8,0},{16,24},{24,16},{32,40},{40,32},{48,56},{56,48},{64,72... | collective-permute-start | bytes 1572872 | tf_op jit(solution)/shard_map/ppermute | solution.py:29
  87.0 0.0 collective-permute-done.11.refs_6_
  87.0 5.2 %collective-permute-start.12 = (bf16[512,512]{1,0:T(8,128)(2,1)S(1)}, bf16[512,512]{1,0:T(8,128)(2,1)S(1)}, u32[]{:S(2)}, u32[]{:S(2)}) collective-permute-start(bf16[512,512]{1,0:T(8,128)(2,1)S(1)} %collective-permute-done.11.refs_6_), channel_id=1, source_target_pairs={{0,8},{8,0},{16,24},{24,16},{32,40},{40,32},{48,56},{56,48},{64,72... | collective-permute-start | bytes 1572872 | tf_op jit(solution)/shard_map/ppermute | solution.py:29
  92.2 0.0 collective-permute-done.5.refs_1_
  92.2 0.0 collective-permute-done.9.refs_4_
  92.2 0.0 collective-permute-done.10.refs_5_
  92.2 1.5 %collective-permute-done.12.refs_7_ = bf16[512,512]{1,0:T(8,128)(2,1)S(1)} collective-permute-done((bf16[512,512]{1,0:T(8,128)(2,1)S(1)}, bf16[512,512]{1,0:T(8,128)(2,1)S(1)}, u32[]{:S(2)}, u32[]{:S(2)}) %collective-permute-start.12) | collective-permute-done | bytes 524320 | tf_op jit(solution)/shard_map/ppermute | solution.py:29
  93.7 0.0 copy-done.4
  93.7 0.0 copy-done.6
  93.7 4.1 %shard_map.118 = (bf16[128,512]{1,0:T(8,128)(2,1)}, bf16[128,4096]{1,0:T(8,128)(2,1)}) custom-call(bf16[512,512]{1,0:T(8,128)(2,1)S(1)} %shard_map.116.refs_0_, bf16[512,512]{1,0:T(8,128)(2,1)S(1)} %collective-permute-done.5.refs_1_, bf16[512,512]{1,0:T(8,128)(2,1)S(1)} %shard_map.117.refs_2_, bf16[512,512]{1,0:T(8,128)(2,1)S(1)} %collective-permute-done.8.refs_3_, ...), custom_call_target="tpu_custom_call" | custom-call | flops 1073741824 | bytes 8388608 | tf_op jit(solution)/shard_map/pallas_call | solution.py:240
  (5 shorter events, 0.1 us)
Async XLA Ops:
  0.6 20.6 %collective-permute-start.1 = (bf16[32,512]{1,0:T(8,128)(2,1)}, bf16[32,512]{1,0:T(8,128)(2,1)S(1)}, u32[]{:S(2)}, u32[]{:S(2)}) collective-permute-start(bf16[32,512]{1,0:T(8,128)(2,1)} %bitcast.12), channel_id=1, source_target_pairs={{8,504},{24,8},{40,24},{56,40},{72,56},{88,72},{104,88},{120,104},... | collective-permute-start | bytes 98312 | tf_op jit(solution)/shard_map/ppermute | solution.py:62
  19.9 3.6 %collective-permute-start = (bf16[32,512]{1,0:T(8,128)(2,1)}, bf16[32,512]{1,0:T(8,128)(2,1)S(1)}, u32[]{:S(2)}, u32[]{:S(2)}) collective-permute-start(bf16[32,512]{1,0:T(8,128)(2,1)} %bitcast.13), channel_id=1, source_target_pairs={{0,504},{8,0},{16,8},{24,16},{32,24},{40,32},{48,40},{56,48},{64,5... | collective-permute-start | bytes 98312 | tf_op jit(solution)/shard_map/ppermute | solution.py:29
  23.4 0.8 copy-start.5
  24.2 18.1 %collective-permute-start.2 = (bf16[64,512]{1,0:T(8,128)(2,1)S(1)}, bf16[64,512]{1,0:T(8,128)(2,1)S(1)}, u32[]{:S(2)}, u32[]{:S(2)}) collective-permute-start(bf16[64,512]{1,0:T(8,128)(2,1)S(1)} %shard_map.111.first.ahead), channel_id=1, source_target_pairs={{0,128},{8,392},{16,144},{24,408},{32,160},{40,424},{48,176},{56,4... | collective-permute-start | bytes 196616 | tf_op jit(solution)/shard_map/ppermute | solution.py:29
  33.0 1.0 %copy-start.1 = (f32[16,8192]{1,0:T(8,128)S(1)}, f32[16,8192]{1,0:T(8,128)}, u32[]{:S(2)}) copy-start(f32[16,8192]{1,0:T(8,128)} %params.1) | copy-start | bytes 1572868
  34.0 1.0 %copy-start.2 = (f32[1,16,8192]{2,1,0:T(8,128)S(1)}, f32[1,16,8192]{2,1,0:T(8,128)}, u32[]{:S(2)}) copy-start(f32[1,16,8192]{2,1,0:T(8,128)} %param.13) | copy-start | bytes 1572868
  35.1 1.0 %copy-start.3 = (f32[16,8192]{1,0:T(8,128)S(1)}, f32[16,8192]{1,0:T(8,128)}, u32[]{:S(2)}) copy-start(f32[16,8192]{1,0:T(8,128)} %momentum.1) | copy-start | bytes 1572868
  37.2 11.2 %all-to-all-start = ((f32[8,64,128]{2,1,0:T(8,128)}), f32[8,64,128]{2,1,0:T(8,128)S(1)}, u32[]{:S(2)}, u32[]{:S(2)}) async-start(f32[8,64,128]{2,1,0:T(8,128)} %get-tuple-element.12), calls=%async_computation | async-start | bytes 524288 | tf_op jit(solution)/shard_map/all_to_all | solution.py:212
  42.2 6.1 %copy-start = (bf16[1,128,4096]{2,1,0:T(8,128)(2,1)S(1)}, bf16[1,128,4096]{2,1,0:T(8,128)(2,1)}, u32[]{:S(2)}) copy-start(bf16[1,128,4096]{2,1,0:T(8,128)(2,1)} %param.8) | copy-start | bytes 3145732
  42.3 12.5 %collective-permute-start.3 = (bf16[128,512]{1,0:T(8,128)(2,1)S(1)}, bf16[128,512]{1,0:T(8,128)(2,1)S(1)}, u32[]{:S(2)}, u32[]{:S(2)}) collective-permute-start(bf16[128,512]{1,0:T(8,128)(2,1)S(1)} %shard_map.112.first), channel_id=1, source_target_pairs={{0,64},{8,456},{16,80},{24,472},{32,96},{40,488},{48,112},{56,504}... | collective-permute-start | bytes 393224 | tf_op jit(solution)/shard_map/ppermute | solution.py:29
  54.8 11.1 %collective-permute-start.4 = (bf16[256,512]{1,0:T(8,128)(2,1)S(1)}, bf16[256,512]{1,0:T(8,128)(2,1)S(1)}, u32[]{:S(2)}, u32[]{:S(2)}) collective-permute-start(bf16[256,512]{1,0:T(8,128)(2,1)S(1)} %shard_map.115.first), channel_id=1, source_target_pairs={{0,32},{8,488},{16,48},{24,504},{32,64},{40,8},{48,80},{56,24},{64... | collective-permute-start | bytes 786440 | tf_op jit(solution)/shard_map/ppermute | solution.py:29
  56.7 17.2 %collective-permute-start.6 = (bf16[256,512]{1,0:T(8,128)(2,1)S(1)}, bf16[256,512]{1,0:T(8,128)(2,1)S(1)}, u32[]{:S(2)}, u32[]{:S(2)}) collective-permute-start(bf16[256,512]{1,0:T(8,128)(2,1)S(1)} %shard_map.115.first), channel_id=1, source_target_pairs={{0,512},{8,520},{16,528},{24,536},{32,544},{40,552},{48,560},{56,5... | collective-permute-start | bytes 786440 | tf_op jit(solution)/shard_map/ppermute | solution.py:29
  65.9 10.4 %collective-permute-start.7 = (bf16[256,512]{1,0:T(8,128)(2,1)S(1)}, bf16[256,512]{1,0:T(8,128)(2,1)S(1)}, u32[]{:S(2)}, u32[]{:S(2)}) collective-permute-start(bf16[256,512]{1,0:T(8,128)(2,1)S(1)} %collective-permute-done.4.second), channel_id=1, source_target_pairs={{0,512},{8,520},{16,528},{24,536},{32,544},{40,552},{48,560},{56,5... | collective-permute-start | bytes 786440 | tf_op jit(solution)/shard_map/ppermute | solution.py:29
  70.4 23.3 %copy-start.4 = (bf16[1,128,512]{2,1,0:T(8,128)(2,1)S(1)}, bf16[1,128,512]{2,1,0:T(8,128)(2,1)}, u32[]{:S(2)}) copy-start(bf16[1,128,512]{2,1,0:T(8,128)(2,1)} %param.11) | copy-start | bytes 393220
  70.4 23.3 %copy-start.6 = (bf16[1,4096]{1,0:T(2,128)(2,1)S(1)}, bf16[1,4096]{1,0:T(2,128)(2,1)}, u32[]{:S(2)}) copy-start(bf16[1,4096]{1,0:T(2,128)(2,1)} %refs_10_.1) | copy-start | bytes 24580
  70.4 14.6 %collective-permute-start.8 = (bf16[512,512]{1,0:T(8,128)(2,1)S(1)}, bf16[512,512]{1,0:T(8,128)(2,1)S(1)}, u32[]{:S(2)}, u32[]{:S(2)}) collective-permute-start(bf16[512,512]{1,0:T(8,128)(2,1)S(1)} %shard_map.116.refs_0_), channel_id=1, source_target_pairs={{0,16},{8,504},{16,32},{24,8},{32,48},{40,24},{48,64},{56,40},{64,... | collective-permute-start | bytes 1572872 | tf_op jit(solution)/shard_map/ppermute | solution.py:29
  76.3 10.7 %collective-permute-start.11 = (bf16[512,512]{1,0:T(8,128)(2,1)S(1)}, bf16[512,512]{1,0:T(8,128)(2,1)S(1)}, u32[]{:S(2)}, u32[]{:S(2)}) collective-permute-start(bf16[512,512]{1,0:T(8,128)(2,1)S(1)} %shard_map.117.refs_2_), channel_id=1, source_target_pairs={{0,16},{8,504},{16,32},{24,8},{32,48},{40,24},{48,64},{56,40},{64,... | collective-permute-start | bytes 1572872 | tf_op jit(solution)/shard_map/ppermute | solution.py:29
  80.7 11.5 %collective-permute-start.5 = (bf16[512,512]{1,0:T(8,128)(2,1)S(1)}, bf16[512,512]{1,0:T(8,128)(2,1)S(1)}, u32[]{:S(2)}, u32[]{:S(2)}) collective-permute-start(bf16[512,512]{1,0:T(8,128)(2,1)S(1)} %shard_map.116.refs_0_), channel_id=1, source_target_pairs={{0,8},{8,0},{16,24},{24,16},{32,40},{40,32},{48,56},{56,48},{64,72... | collective-permute-start | bytes 1572872 | tf_op jit(solution)/shard_map/ppermute | solution.py:29
  82.6 9.6 %collective-permute-start.9 = (bf16[512,512]{1,0:T(8,128)(2,1)S(1)}, bf16[512,512]{1,0:T(8,128)(2,1)S(1)}, u32[]{:S(2)}, u32[]{:S(2)}) collective-permute-start(bf16[512,512]{1,0:T(8,128)(2,1)S(1)} %shard_map.117.refs_2_), channel_id=1, source_target_pairs={{0,8},{8,0},{16,24},{24,16},{32,40},{40,32},{48,56},{56,48},{64,72... | collective-permute-start | bytes 1572872 | tf_op jit(solution)/shard_map/ppermute | solution.py:29
  85.0 7.2 %collective-permute-start.10 = (bf16[512,512]{1,0:T(8,128)(2,1)S(1)}, bf16[512,512]{1,0:T(8,128)(2,1)S(1)}, u32[]{:S(2)}, u32[]{:S(2)}) collective-permute-start(bf16[512,512]{1,0:T(8,128)(2,1)S(1)} %collective-permute-done.8.refs_3_), channel_id=1, source_target_pairs={{0,8},{8,0},{16,24},{24,16},{32,40},{40,32},{48,56},{56,48},{64,72... | collective-permute-start | bytes 1572872 | tf_op jit(solution)/shard_map/ppermute | solution.py:29
  87.0 6.7 %collective-permute-start.12 = (bf16[512,512]{1,0:T(8,128)(2,1)S(1)}, bf16[512,512]{1,0:T(8,128)(2,1)S(1)}, u32[]{:S(2)}, u32[]{:S(2)}) collective-permute-start(bf16[512,512]{1,0:T(8,128)(2,1)S(1)} %collective-permute-done.11.refs_6_), channel_id=1, source_target_pairs={{0,8},{8,0},{16,24},{24,16},{32,40},{40,32},{48,56},{56,48},{64,72... | collective-permute-start | bytes 1572872 | tf_op jit(solution)/shard_map/ppermute | solution.py:29

commit v3 on v2

--- a/solution.py
+++ b/solution.py
@@ -41,13 +41,13 @@
     return send(array, lambda y, z, c: (y, z, 1 - c))
 
 
-def chip_kernel(own, first, second, out):
-    rows = own.shape[0]
+def chip_kernel(first, second, out):
+    rows = first.shape[0]
     core = lax.rem(lax.axis_index("fsdp"), C)
 
     @pl.when(core == 0)
     def _():
-        out[:rows, :] = own[...]
+        out[:rows, :] = second[...]
         out[rows:, :] = first[...]
 
     @pl.when(core != 0)
@@ -58,16 +58,15 @@
 
 def chip_rows(own):
     first = send(own, lambda y, z, c: (y, z - 1, 1) if c == 0 else (y, z, 0))
-    down = [(at(y, z, c), at(y, z - 1, c)) for y, z, c in sources() if c == 1]
-    second = lax.ppermute(own, "fsdp", down)
+    second = send(own, lambda y, z, c: (y, z - c, c))
     rows, width = own.shape
     return pl.pallas_call(
         chip_kernel,
         out_shape=jax.ShapeDtypeStruct((C * rows, width), own.dtype),
-        in_specs=[VMEM] * 3,
+        in_specs=[VMEM] * 2,
         out_specs=VMEM,
         compiler_params=pltpu.CompilerParams(vmem_limit_bytes=2**20),
-    )(own, first, second)
+    )(first, second)
 
 
 def join_kernel(first, second, *refs):
@@ -123,7 +122,7 @@
         in_specs=[SMEM] + [ANY] * 4,
         out_specs=(VMEM,) * 3,
         scratch_shapes=[pltpu.VMEM((3, 8, length), jnp.float32), pltpu.SemaphoreType.DMA((3,))],
-        compiler_params=pltpu.CompilerParams(vmem_limit_bytes=4 * 2**20),
+        compiler_params=pltpu.CompilerParams(vmem_limit_bytes=60 * 2**20),
     )(fragment, params, local, momentum, ahead)
 
 
@@ -155,49 +154,74 @@
     )(everyone, params_row, moment_row, tokens)
 
 
-def layer_kernel(rows, layout, *refs):
+def position():
+    place = lax.axis_index("fsdp")
+    chip = lax.div(place, C)
+    return lax.div(chip, Z), lax.rem(chip, Z), lax.rem(place, C)
+
+
+def put(piece, full, rows, other_core, offsets):
+    _, z, core = position()
+    owner_core = 1 - core if other_core else core
+    for slot, moved in enumerate(offsets):
+        owner_z = lax.rem(z + Z + jnp.where(owner_core == 0, -moved, moved + 1), Z)
+        start = pl.multiple_of(owner_z * rows, rows)
+        full[pl.ds(start, rows), :] = piece[slot * rows : (slot + 1) * rows, :]
+
+
+def lanes_of(column, half, first, chunk):
+    return pl.ds(pl.multiple_of(column * half + first, 128), chunk)
+
+
+CHUNK = 512
+
+
+def forward(tokens, inv, gain, full, column, total):
+    for first in range(0, full.shape[0], CHUNK):
+        lanes = lanes_of(column, full.shape[0], first, CHUNK)
+        unit = tokens[:, lanes].astype(jnp.float32) * inv[...]
+        normed = (unit * gain[:, lanes].astype(jnp.float32)).astype(jnp.bfloat16)
+        total += jnp.dot(normed, full[first : first + CHUNK, :], preferred_element_type=jnp.float32)
+    return total
+
+
+def gained_of(upstream, gain, full, column, first):
+    grad = lax.dot_general(
+        upstream, full[first : first + CHUNK, :], (((1,), (1,)), ((), ())), preferred_element_type=jnp.float32
+    )
+    return grad * gain[:, lanes_of(column, full.shape[0], first, CHUNK)].astype(jnp.float32)
+
+
+def own_kernel(rows, layout, *refs):
     pieces = refs[: len(layout)]
-    tokens, inv, gain, cotangent, projected, token_grad, full, staged, upstream, sems = refs[len(layout) :]
-    fetch = pltpu.make_async_copy(cotangent, upstream, sems.at[len(layout)])
-    fetch.start()
-    loads, first = [], 0
-    for number, piece in enumerate(pieces):
-        target = staged.at[pl.ds(first, piece.shape[0])]
-        loads.append((first, pltpu.make_async_copy(piece, target, sems.at[number])))
-        loads[-1][1].start()
-        first += piece.shape[0]
-    place = lax.axis_index("fsdp")
-    core = lax.rem(place, C)
-    chip = lax.div(place, C)
-    z, y = lax.rem(chip, Z), lax.div(chip, Z)
-    for (first, load), (other_y, other_core, offsets) in zip(loads, layout):
-        owner_y = 1 - y if other_y else y
-        owner_core = 1 - core if other_core else core
-        load.wait()
-        for slot, moved in enumerate(offsets):
-            owner_z = lax.rem(z + Z + jnp.where(owner_core == 0, -moved, moved + 1), Z)
-            start = pl.multiple_of((owner_y * Z + owner_z) * rows, rows)
-            full[pl.ds(start, rows), :] = staged[first + slot * rows : first + (slot + 1) * rows, :]
-    features = full.shape[0]
-    chunk = 512
-    total = jnp.zeros(projected.shape, jnp.float32)
-    for first in range(0, features, chunk):
-        cols = slice(first, first + chunk)
-        unit = tokens[:, cols].astype(jnp.float32) * inv[...]
-        normed = (unit * gain[:, cols].astype(jnp.float32)).astype(jnp.bfloat16)
-        total += jnp.dot(normed, full[cols, :], preferred_element_type=jnp.float32)
+    tokens, inv, gain, upstream, partial, gained, full = refs[len(layout) :]
+    for piece, (other_core, offsets) in zip(pieces, layout):
+        put(piece, full, rows, other_core, offsets)
+    y, _, _ = position()
+    partial[...] = forward(tokens, inv, gain, full, y, jnp.zeros(partial.shape, jnp.float32))
+    for first in range(0, full.shape[0], CHUNK):
+        gained[:, first : first + CHUNK] = gained_of(upstream[...], gain, full, y, first)
+
+
+def other_kernel(rows, layout, *refs):
+    pieces = refs[: len(layout)]
+    tokens, inv, gain, upstream, partial, gained, projected, token_grad, full = refs[len(layout) :]
+    for piece, (other_core, offsets) in zip(pieces, layout):
+        put(piece, full, rows, other_core, offsets)
+    y, _, _ = position()
+    total = forward(tokens, inv, gain, full, 1 - y, partial[...])
     projected[...] = total.astype(jnp.bfloat16)
-    fetch.wait()
     above = upstream[...]
-    inner = jnp.sum(above.astype(jnp.float32) * total, axis=1, keepdims=True) / features
-    for first in range(0, features, chunk):
-        cols = slice(first, first + chunk)
-        grad = lax.dot_general(
-            above, full[cols, :], (((1,), (1,)), ((), ())), preferred_element_type=jnp.float32
-        )
-        unit = tokens[:, cols].astype(jnp.float32) * inv[...]
-        gained = grad * gain[:, cols].astype(jnp.float32)
-        token_grad[:, cols] = (inv[...] * (gained - unit * inner)).astype(jnp.bfloat16)
+    inner = jnp.sum(above.astype(jnp.float32) * total, axis=1, keepdims=True) / tokens.shape[1]
+
+    def finish(column, first, values):
+        lanes = lanes_of(column, full.shape[0], first, CHUNK)
+        unit = tokens[:, lanes].astype(jnp.float32) * inv[...]
+        token_grad[:, lanes] = (inv[...] * (values - unit * inner)).astype(jnp.bfloat16)
+
+    for first in range(0, full.shape[0], CHUNK):
+        finish(1 - y, first, gained_of(above, gain, full, 1 - y, first))
+        finish(y, first, gained[:, first : first + CHUNK])
 
 
 def shards(tokens, norm_gain, weight, cotangent, global_params, local_params, momentum, fragment):
@@ -224,36 +248,41 @@
     last_y = along_z(eight_y, 1)
     before = (0, 8, 4, 12, 2, 10, 6, 14)
     after = tuple(moved + 1 for moved in before)
-    gathered = [
-        (eight, False, False, before),
-        (eight_c, False, True, before),
-        (eight_y, True, False, before),
-        (last, False, False, after),
-        (across_core(eight_y), True, True, before),
-        (across_core(last), False, True, after),
-        (last_y, True, False, after),
-        (across_core(last_y), True, True, after),
-    ]
-    layout = [entry[1:] for entry in gathered]
     count, features = block.shape
     width = own.shape[1]
+    half = features // Y
+    layout = [(False, before), (True, before), (False, after), (True, after)]
+    scratch = [pltpu.VMEM((half, width), jnp.bfloat16)]
+    params = pltpu.CompilerParams(vmem_limit_bytes=8 * 2**20)
+    flops = 2 * count * features * width
+    cost = pl.CostEstimate(flops=flops, bytes_accessed=4 * 2**20, transcendentals=0)
+    partial, gained = pl.pallas_call(
+        functools.partial(own_kernel, rows, layout),
+        out_shape=(
+            jax.ShapeDtypeStruct((count, width), jnp.float32),
+            jax.ShapeDtypeStruct((count, half), jnp.float32),
+        ),
+        in_specs=[VMEM] * (len(layout) + 4),
+        out_specs=(VMEM, VMEM),
+        scratch_shapes=scratch,
+        compiler_params=params,
+        cost_estimate=cost,
+    )(eight, eight_c, last, across_core(last), block, inv, norm_gain, cotangent[0])
     projected, token_grad = pl.pallas_call(
-        functools.partial(layer_kernel, rows, layout),
+        functools.partial(other_kernel, rows, layout),
         out_shape=(
             jax.ShapeDtypeStruct((count, width), jnp.bfloat16),
             jax.ShapeDtypeStruct((count, features), jnp.bfloat16),
         ),
-        in_specs=[ANY] * len(layout) + [VMEM] * 3 + [ANY],
+        in_specs=[VMEM] * (len(layout) + 6),
         out_specs=(VMEM, VMEM),
-        scratch_shapes=[
-            pltpu.VMEM((features, width), jnp.bfloat16),
-            pltpu.VMEM((features, width), jnp.bfloat16),
-            pltpu.VMEM((count, width), jnp.bfloat16),
-            pltpu.SemaphoreType.DMA((len(layout) + 1,)),
-        ],
-        compiler_params=pltpu.CompilerParams(vmem_limit_bytes=16 * 2**20),
-        cost_estimate=pl.CostEstimate(flops=4 * count * features * width, bytes_accessed=8 * 2**20, transcendentals=0),
-    )(*[entry[0] for entry in gathered], block, inv, norm_gain, cotangent[0])
+        scratch_shapes=scratch,
+        compiler_params=params,
+        cost_estimate=cost,
+    )(
+        *(eight_y, across_core(eight_y), last_y, across_core(last_y)),
+        *(block, inv, norm_gain, cotangent[0], partial, gained),
+    )
     return (projected[None], token_grad[None], global_next.reshape(-1), momentum_next.reshape(-1))
 
 

time: 98.6 us -> 97.3 us (0.987)
  starting transfers between devices: 68 us -> 72.8 us
  waiting for transfers between devices: 18.3 us -> 13.9 us
  local copies, waits for them, and re-layouts: 3.89 us -> 0.03 us
  Pallas kernels: 6.12 us -> 8.37 us
    ppermute x12 -> x13, starting transfers between devices: 43.8 us -> 67.7 us  [send(): lax.ppermute(array, 'fsdp', [(at(*here), at(*step(*here))) for here in so...]
    ppermute x1 -> x0, starting transfers between devices: 19.2 us -> none  [chip_rows(): second = lax.ppermute(own, 'fsdp', down)]
    unnamed x14 -> x10, local copies, waits for them, and re-layouts: 3.89 us -> 0.03 us
    ppermute x12 -> x13, waiting for transfers between devices: 16.2 us -> 13.9 us  [send(): lax.ppermute(array, 'fsdp', [(at(*here), at(*step(*here))) for here in so...]
    ppermute x1 -> x0, waiting for transfers between devices: 1.29 us -> none  [chip_rows(): second = lax.ppermute(own, 'fsdp', down)]
    pallas_call x1, Pallas kernels: 1.05 us -> 2.16 us  [pick(): pl.pallas_call(pick_kernel, out_shape=(jax.ShapeDtypeStruct((replicas, li...]
    pallas_call x1 -> x2, Pallas kernels: 4.13 us -> 3.7 us  [the longest x1 2.41 us: shards(): pl.pallas_call(functools.partial(other_kernel, rows, layout), out_shape=(...]
  transfers between devices with their start and end apart: 14 -> 14, of which waited for: 7 -> 5; matrix products, arithmetic and copies ran while one was open for 0% -> 0% of each run, Pallas kernels for 2% -> 5%
where the time goes in v3:
time: 97.3 us; the launch traced here: 96.7 us
  starting transfers between devices  72.8 us (75%)
  waiting for transfers between devices  13.9 us (14%)
  Pallas kernels  8.37 us (9%)
  between operations  1.57 us (2%)
    ppermute x13, starting transfers between devices, send(): lax.ppermute(array, 'fsdp', [(at(*here), at(*step(*here))) for here in so...  67.7 us
    ppermute x13, waiting for transfers between devices, send(): lax.ppermute(array, 'fsdp', [(at(*here), at(*step(*here))) for here in so...  13.9 us
    all_to_all x1, starting transfers between devices, shards(): everyone = lax.all_to_all(spread, 'replica', 0, 0)  5.04 us
    pallas_call x1, Pallas kernels, shards(): pl.pallas_call(functools.partial(other_kernel, rows, layout), out_shape=(...  2.41 us
    pallas_call x1, Pallas kernels, pick(): pl.pallas_call(pick_kernel, out_shape=(jax.ShapeDtypeStruct((replicas, li...  2.16 us
  transfers between devices with their start and end apart: 14, of which 5 were waited for; matrix products, arithmetic and copies ran while one was open for 0% of the time, Pallas kernels for 5%

profile of v3, /device:TPU:1, one launch (start us, length us, event | category | flops | bytes accessed | tf_op | source)
XLA Modules:
  0.0 96.7 jit_solution(11331334096920829541)
XLA Ops:
  0.6 19.2 %collective-permute-start.1 = (bf16[32,512]{1,0:T(8,128)(2,1)}, bf16[32,512]{1,0:T(8,128)(2,1)S(1)}, u32[]{:S(2)}, u32[]{:S(2)}) collective-permute-start(bf16[32,512]{1,0:T(8,128)(2,1)} %bitcast.16), channel_id=1, source_target_pairs={{0,0},{8,504},{16,16},{24,8},{32,32},{40,24},{48,48},{56,40},{64,6... | collective-permute-start | bytes 98312 | tf_op jit(solution)/shard_map/ppermute | solution.py:29
  19.9 0.0 collective-permute-start
  19.9 1.3 %collective-permute-done.1.second = bf16[32,512]{1,0:T(8,128)(2,1)S(1)} collective-permute-done((bf16[32,512]{1,0:T(8,128)(2,1)}, bf16[32,512]{1,0:T(8,128)(2,1)S(1)}, u32[]{:S(2)}, u32[]{:S(2)}) %collective-permute-start.1) | collective-permute-done | bytes 32800 | tf_op jit(solution)/shard_map/ppermute | solution.py:29
  21.2 2.2 %collective-permute-done.first = bf16[32,512]{1,0:T(8,128)(2,1)S(1)} collective-permute-done((bf16[32,512]{1,0:T(8,128)(2,1)}, bf16[32,512]{1,0:T(8,128)(2,1)S(1)}, u32[]{:S(2)}, u32[]{:S(2)}) %collective-permute-start) | collective-permute-done | bytes 32800 | tf_op jit(solution)/shard_map/ppermute | solution.py:29
  23.4 0.6 shard_map.111.first.ahead
  24.1 8.2 %collective-permute-start.2 = (bf16[64,512]{1,0:T(8,128)(2,1)}, bf16[64,512]{1,0:T(8,128)(2,1)S(1)}, u32[]{:S(2)}, u32[]{:S(2)}) collective-permute-start(bf16[64,512]{1,0:T(8,128)(2,1)} %shard_map.111.first.ahead), channel_id=1, source_target_pairs={{0,128},{8,392},{16,144},{24,408},{32,160},{40,424},{48,176},{56,4... | collective-permute-start | bytes 196616 | tf_op jit(solution)/shard_map/ppermute | solution.py:29
  32.9 2.2 %shard_map.113 = (f32[8,64,128]{2,1,0:T(8,128)}, f32[64,128]{1,0:T(8,128)}, f32[64,128]{1,0:T(8,128)}) custom-call(s32[1]{0:T(128)S(6)} %copy.12.chosen, f32[16,8192]{1,0:T(8,128)} %params.1, f32[16,8192]{1,0:T(8,128)} %bitcast.13, f32[16,8192]{1,0:T(8,128)} %momentum.1, bf16[64,512]{1,0:T(8,128)(2,1)} %shard_map.111.first.ahead), custom_call_target="tpu_custom_call" | custom-call | tf_op jit(solution)/shard_map/pallas_call | solution.py:119
  35.0 5.0 %all-to-all-start = ((f32[8,64,128]{2,1,0:T(8,128)}), f32[8,64,128]{2,1,0:T(8,128)S(1)}, u32[]{:S(2)}, u32[]{:S(2)}) async-start(f32[8,64,128]{2,1,0:T(8,128)} %get-tuple-element.14), calls=%async_computation | async-start | bytes 524288 | tf_op jit(solution)/shard_map/all_to_all | solution.py:236
  40.1 0.0 copy-start
  40.1 0.0 copy-start.3
  40.1 0.0 copy-start.4
  40.1 0.0 collective-permute-done.2.second
  40.1 0.9 shard_map.112.first
  41.1 5.2 %collective-permute-start.3 = (bf16[128,512]{1,0:T(8,128)(2,1)S(1)}, bf16[128,512]{1,0:T(8,128)(2,1)S(1)}, u32[]{:S(2)}, u32[]{:S(2)}) collective-permute-start(bf16[128,512]{1,0:T(8,128)(2,1)S(1)} %shard_map.112.first), channel_id=1, source_target_pairs={{0,64},{8,456},{16,80},{24,472},{32,96},{40,488},{48,112},{56,504}... | collective-permute-start | bytes 393224 | tf_op jit(solution)/shard_map/ppermute | solution.py:29
  46.3 0.0 all-to-all-done.everyone
  46.3 0.0 copy-done
  46.3 0.0 copy-done.3
  46.3 0.0 copy-done.4
  46.3 0.8 shard_map.114
  47.1 6.0 %collective-permute-done.3.second = bf16[128,512]{1,0:T(8,128)(2,1)S(1)} collective-permute-done((bf16[128,512]{1,0:T(8,128)(2,1)S(1)}, bf16[128,512]{1,0:T(8,128)(2,1)S(1)}, u32[]{:S(2)}, u32[]{:S(2)}) %collective-permute-start.3) | collective-permute-done | bytes 131104 | tf_op jit(solution)/shard_map/ppermute | solution.py:29
  53.2 1.9 %collective-permute-start.5 = (bf16[256,512]{1,0:T(8,128)(2,1)S(1)}, bf16[256,512]{1,0:T(8,128)(2,1)S(1)}, u32[]{:S(2)}, u32[]{:S(2)}) collective-permute-start(bf16[256,512]{1,0:T(8,128)(2,1)S(1)} %shard_map.115.first), channel_id=1, source_target_pairs={{0,32},{8,488},{16,48},{24,504},{32,64},{40,8},{48,80},{56,24},{64... | collective-permute-start | bytes 786440 | tf_op jit(solution)/shard_map/ppermute | solution.py:29
  55.1 5.0 %collective-permute-start.4 = (bf16[256,512]{1,0:T(8,128)(2,1)S(1)}, bf16[256,512]{1,0:T(8,128)(2,1)S(1)}, u32[]{:S(2)}, u32[]{:S(2)}) collective-permute-start(bf16[256,512]{1,0:T(8,128)(2,1)S(1)} %shard_map.115.first), channel_id=1, source_target_pairs={{0,512},{8,520},{16,528},{24,536},{32,544},{40,552},{48,560},{56,5... | collective-permute-start | bytes 786440 | tf_op jit(solution)/shard_map/ppermute | solution.py:29
  60.1 4.2 %collective-permute-done.5.second = bf16[256,512]{1,0:T(8,128)(2,1)S(1)} collective-permute-done((bf16[256,512]{1,0:T(8,128)(2,1)S(1)}, bf16[256,512]{1,0:T(8,128)(2,1)S(1)}, u32[]{:S(2)}, u32[]{:S(2)}) %collective-permute-start.5) | collective-permute-done | bytes 262176 | tf_op jit(solution)/shard_map/ppermute | solution.py:29
  64.3 4.9 %collective-permute-start.6 = (bf16[256,512]{1,0:T(8,128)(2,1)S(1)}, bf16[256,512]{1,0:T(8,128)(2,1)S(1)}, u32[]{:S(2)}, u32[]{:S(2)}) collective-permute-start(bf16[256,512]{1,0:T(8,128)(2,1)S(1)} %collective-permute-done.5.second), channel_id=1, source_target_pairs={{0,512},{8,520},{16,528},{24,536},{32,544},{40,552},{48,560},{56,5... | collective-permute-start | bytes 786440 | tf_op jit(solution)/shard_map/ppermute | solution.py:29
  69.3 0.0 copy-start.1
  69.3 0.0 copy-start.2
  69.3 4.5 %collective-permute-start.11 = (bf16[512,512]{1,0:T(8,128)(2,1)S(1)}, bf16[512,512]{1,0:T(8,128)(2,1)S(1)}, u32[]{:S(2)}, u32[]{:S(2)}) collective-permute-start(bf16[512,512]{1,0:T(8,128)(2,1)S(1)} %shard_map.117.refs_0_), channel_id=1, source_target_pairs={{0,16},{8,504},{16,32},{24,8},{32,48},{40,24},{48,64},{56,40},{64,... | collective-permute-start | bytes 1572872 | tf_op jit(solution)/shard_map/ppermute | solution.py:29
  73.8 0.0 collective-permute-done.4.first
  73.8 0.0 collective-permute-done.6.second
  73.8 5.6 %collective-permute-start.8 = (bf16[512,512]{1,0:T(8,128)(2,1)S(1)}, bf16[512,512]{1,0:T(8,128)(2,1)S(1)}, u32[]{:S(2)}, u32[]{:S(2)}) collective-permute-start(bf16[512,512]{1,0:T(8,128)(2,1)S(1)} %shard_map.116.refs_0_), channel_id=1, source_target_pairs={{0,16},{8,504},{16,32},{24,8},{32,48},{40,24},{48,64},{56,40},{64,... | collective-permute-start | bytes 1572872 | tf_op jit(solution)/shard_map/ppermute | solution.py:29
  79.4 2.8 %collective-permute-start.10 = (bf16[512,512]{1,0:T(8,128)(2,1)S(1)}, bf16[512,512]{1,0:T(8,128)(2,1)S(1)}, u32[]{:S(2)}, u32[]{:S(2)}) collective-permute-start(bf16[512,512]{1,0:T(8,128)(2,1)S(1)} %shard_map.117.refs_0_), channel_id=1, source_target_pairs={{0,8},{8,0},{16,24},{24,16},{32,40},{40,32},{48,56},{56,48},{64,72... | collective-permute-start | bytes 1572872 | tf_op jit(solution)/shard_map/ppermute | solution.py:29
  82.3 0.0 collective-permute-done.11.refs_2_
  82.3 4.8 %collective-permute-start.12 = (bf16[512,512]{1,0:T(8,128)(2,1)S(1)}, bf16[512,512]{1,0:T(8,128)(2,1)S(1)}, u32[]{:S(2)}, u32[]{:S(2)}) collective-permute-start(bf16[512,512]{1,0:T(8,128)(2,1)S(1)} %collective-permute-done.11.refs_2_), channel_id=1, source_target_pairs={{0,8},{8,0},{16,24},{24,16},{32,40},{40,32},{48,56},{56,48},{64,72... | collective-permute-start | bytes 1572872 | tf_op jit(solution)/shard_map/ppermute | solution.py:29
  87.1 1.9 %collective-permute-start.7 = (bf16[512,512]{1,0:T(8,128)(2,1)S(1)}, bf16[512,512]{1,0:T(8,128)(2,1)S(1)}, u32[]{:S(2)}, u32[]{:S(2)}) collective-permute-start(bf16[512,512]{1,0:T(8,128)(2,1)S(1)} %shard_map.116.refs_0_), channel_id=1, source_target_pairs={{0,8},{8,0},{16,24},{24,16},{32,40},{40,32},{48,56},{56,48},{64,72... | collective-permute-start | bytes 1572872 | tf_op jit(solution)/shard_map/ppermute | solution.py:29
  89.0 0.0 collective-permute-done.8.refs_2_
  89.1 3.7 %collective-permute-start.9 = (bf16[512,512]{1,0:T(8,128)(2,1)S(1)}, bf16[512,512]{1,0:T(8,128)(2,1)S(1)}, u32[]{:S(2)}, u32[]{:S(2)}) collective-permute-start(bf16[512,512]{1,0:T(8,128)(2,1)S(1)} %collective-permute-done.8.refs_2_), channel_id=1, source_target_pairs={{0,8},{8,0},{16,24},{24,16},{32,40},{40,32},{48,56},{56,48},{64,72... | collective-permute-start | bytes 1572872 | tf_op jit(solution)/shard_map/ppermute | solution.py:29
  92.7 0.0 collective-permute-done.10.refs_1_
  92.7 0.0 collective-permute-done.12.refs_3_
  92.8 0.0 copy-done.1
  92.8 0.0 copy-done.2
  92.8 1.3 %shard_map.118 = (f32[128,512]{1,0:T(8,128)S(1)}, f32[128,2048]{1,0:T(8,128)S(1)}) custom-call(bf16[512,512]{1,0:T(8,128)(2,1)S(1)} %shard_map.117.refs_0_, bf16[512,512]{1,0:T(8,128)(2,1)S(1)} %collective-permute-done.10.refs_1_, bf16[512,512]{1,0:T(8,128)(2,1)S(1)} %collective-permute-done.11.refs_2_, ...), custom_call_target="tpu_custom_call" | custom-call | flops 536870912 | bytes 4194304 | tf_op jit(solution)/shard_map/pallas_call | solution.py:259
  94.1 0.0 collective-permute-done.7.refs_1_
  94.1 0.2 collective-permute-done.9.refs_3_
  94.2 2.4 %shard_map.119 = (bf16[128,512]{1,0:T(8,128)(2,1)}, bf16[128,4096]{1,0:T(8,128)(2,1)}) custom-call(bf16[512,512]{1,0:T(8,128)(2,1)S(1)} %shard_map.116.refs_0_, bf16[512,512]{1,0:T(8,128)(2,1)S(1)} %collective-permute-done.7.refs_1_, bf16[512,512]{1,0:T(8,128)(2,1)S(1)} %collective-permute-done.8.refs_2_, ...), custom_call_target="tpu_custom_call" | custom-call | flops 536870912 | bytes 4194304 | tf_op jit(solution)/shard_map/pallas_call | solution.py:271
  (3 shorter events, 0.1 us)
Async XLA Ops:
  0.6 20.6 %collective-permute-start.1 = (bf16[32,512]{1,0:T(8,128)(2,1)}, bf16[32,512]{1,0:T(8,128)(2,1)S(1)}, u32[]{:S(2)}, u32[]{:S(2)}) collective-permute-start(bf16[32,512]{1,0:T(8,128)(2,1)} %bitcast.16), channel_id=1, source_target_pairs={{0,0},{8,504},{16,16},{24,8},{32,32},{40,24},{48,48},{56,40},{64,6... | collective-permute-start | bytes 98312 | tf_op jit(solution)/shard_map/ppermute | solution.py:29
  19.9 3.6 %collective-permute-start = (bf16[32,512]{1,0:T(8,128)(2,1)}, bf16[32,512]{1,0:T(8,128)(2,1)S(1)}, u32[]{:S(2)}, u32[]{:S(2)}) collective-permute-start(bf16[32,512]{1,0:T(8,128)(2,1)} %bitcast.17), channel_id=1, source_target_pairs={{0,504},{8,0},{16,8},{24,16},{32,24},{40,32},{48,40},{56,48},{64,5... | collective-permute-start | bytes 98312 | tf_op jit(solution)/shard_map/ppermute | solution.py:29
  24.1 16.1 %collective-permute-start.2 = (bf16[64,512]{1,0:T(8,128)(2,1)}, bf16[64,512]{1,0:T(8,128)(2,1)S(1)}, u32[]{:S(2)}, u32[]{:S(2)}) collective-permute-start(bf16[64,512]{1,0:T(8,128)(2,1)} %shard_map.111.first.ahead), channel_id=1, source_target_pairs={{0,128},{8,392},{16,144},{24,408},{32,160},{40,424},{48,176},{56,4... | collective-permute-start | bytes 196616 | tf_op jit(solution)/shard_map/ppermute | solution.py:29
  35.0 11.2 %all-to-all-start = ((f32[8,64,128]{2,1,0:T(8,128)}), f32[8,64,128]{2,1,0:T(8,128)S(1)}, u32[]{:S(2)}, u32[]{:S(2)}) async-start(f32[8,64,128]{2,1,0:T(8,128)} %get-tuple-element.14), calls=%async_computation | async-start | bytes 524288 | tf_op jit(solution)/shard_map/all_to_all | solution.py:236
  40.1 6.2 %copy-start = (bf16[1,128,4096]{2,1,0:T(8,128)(2,1)S(1)}, bf16[1,128,4096]{2,1,0:T(8,128)(2,1)}, u32[]{:S(2)}) copy-start(bf16[1,128,4096]{2,1,0:T(8,128)(2,1)} %param.8) | copy-start | bytes 3145732
  40.1 6.2 %copy-start.3 = (f32[64,128]{1,0:T(8,128)S(1)}, f32[64,128]{1,0:T(8,128)}, u32[]{:S(2)}) copy-start(f32[64,128]{1,0:T(8,128)} %get-tuple-element.15.params_row) | copy-start | bytes 98308
  40.1 6.2 %copy-start.4 = (f32[64,128]{1,0:T(8,128)S(1)}, f32[64,128]{1,0:T(8,128)}, u32[]{:S(2)}) copy-start(f32[64,128]{1,0:T(8,128)} %get-tuple-element.16.moment_row) | copy-start | bytes 98308
  41.1 12.1 %collective-permute-start.3 = (bf16[128,512]{1,0:T(8,128)(2,1)S(1)}, bf16[128,512]{1,0:T(8,128)(2,1)S(1)}, u32[]{:S(2)}, u32[]{:S(2)}) collective-permute-start(bf16[128,512]{1,0:T(8,128)(2,1)S(1)} %shard_map.112.first), channel_id=1, source_target_pairs={{0,64},{8,456},{16,80},{24,472},{32,96},{40,488},{48,112},{56,504}... | collective-permute-start | bytes 393224 | tf_op jit(solution)/shard_map/ppermute | solution.py:29
  53.2 11.1 %collective-permute-start.5 = (bf16[256,512]{1,0:T(8,128)(2,1)S(1)}, bf16[256,512]{1,0:T(8,128)(2,1)S(1)}, u32[]{:S(2)}, u32[]{:S(2)}) collective-permute-start(bf16[256,512]{1,0:T(8,128)(2,1)S(1)} %shard_map.115.first), channel_id=1, source_target_pairs={{0,32},{8,488},{16,48},{24,504},{32,64},{40,8},{48,80},{56,24},{64... | collective-permute-start | bytes 786440 | tf_op jit(solution)/shard_map/ppermute | solution.py:29
  55.1 18.7 %collective-permute-start.4 = (bf16[256,512]{1,0:T(8,128)(2,1)S(1)}, bf16[256,512]{1,0:T(8,128)(2,1)S(1)}, u32[]{:S(2)}, u32[]{:S(2)}) collective-permute-start(bf16[256,512]{1,0:T(8,128)(2,1)S(1)} %shard_map.115.first), channel_id=1, source_target_pairs={{0,512},{8,520},{16,528},{24,536},{32,544},{40,552},{48,560},{56,5... | collective-permute-start | bytes 786440 | tf_op jit(solution)/shard_map/ppermute | solution.py:29
  64.3 9.5 %collective-permute-start.6 = (bf16[256,512]{1,0:T(8,128)(2,1)S(1)}, bf16[256,512]{1,0:T(8,128)(2,1)S(1)}, u32[]{:S(2)}, u32[]{:S(2)}) collective-permute-start(bf16[256,512]{1,0:T(8,128)(2,1)S(1)} %collective-permute-done.5.second), channel_id=1, source_target_pairs={{0,512},{8,520},{16,528},{24,536},{32,544},{40,552},{48,560},{56,5... | collective-permute-start | bytes 786440 | tf_op jit(solution)/shard_map/ppermute | solution.py:29
  69.3 23.5 %copy-start.1 = (bf16[1,128,512]{2,1,0:T(8,128)(2,1)S(1)}, bf16[1,128,512]{2,1,0:T(8,128)(2,1)}, u32[]{:S(2)}) copy-start(bf16[1,128,512]{2,1,0:T(8,128)(2,1)} %param.11) | copy-start | bytes 393220
  69.3 23.5 %copy-start.2 = (bf16[1,4096]{1,0:T(2,128)(2,1)S(1)}, bf16[1,4096]{1,0:T(2,128)(2,1)}, u32[]{:S(2)}) copy-start(bf16[1,4096]{1,0:T(2,128)(2,1)} %refs_6_.3) | copy-start | bytes 24580
  69.3 12.9 %collective-permute-start.11 = (bf16[512,512]{1,0:T(8,128)(2,1)S(1)}, bf16[512,512]{1,0:T(8,128)(2,1)S(1)}, u32[]{:S(2)}, u32[]{:S(2)}) collective-permute-start(bf16[512,512]{1,0:T(8,128)(2,1)S(1)} %shard_map.117.refs_0_), channel_id=1, source_target_pairs={{0,16},{8,504},{16,32},{24,8},{32,48},{40,24},{48,64},{56,40},{64,... | collective-permute-start | bytes 1572872 | tf_op jit(solution)/shard_map/ppermute | solution.py:29
  73.8 15.2 %collective-permute-start.8 = (bf16[512,512]{1,0:T(8,128)(2,1)S(1)}, bf16[512,512]{1,0:T(8,128)(2,1)S(1)}, u32[]{:S(2)}, u32[]{:S(2)}) collective-permute-start(bf16[512,512]{1,0:T(8,128)(2,1)S(1)} %shard_map.116.refs_0_), channel_id=1, source_target_pairs={{0,16},{8,504},{16,32},{24,8},{32,48},{40,24},{48,64},{56,40},{64,... | collective-permute-start | bytes 1572872 | tf_op jit(solution)/shard_map/ppermute | solution.py:29
  79.4 13.3 %collective-permute-start.10 = (bf16[512,512]{1,0:T(8,128)(2,1)S(1)}, bf16[512,512]{1,0:T(8,128)(2,1)S(1)}, u32[]{:S(2)}, u32[]{:S(2)}) collective-permute-start(bf16[512,512]{1,0:T(8,128)(2,1)S(1)} %shard_map.117.refs_0_), channel_id=1, source_target_pairs={{0,8},{8,0},{16,24},{24,16},{32,40},{40,32},{48,56},{56,48},{64,72... | collective-permute-start | bytes 1572872 | tf_op jit(solution)/shard_map/ppermute | solution.py:29
  82.3 10.5 %collective-permute-start.12 = (bf16[512,512]{1,0:T(8,128)(2,1)S(1)}, bf16[512,512]{1,0:T(8,128)(2,1)S(1)}, u32[]{:S(2)}, u32[]{:S(2)}) collective-permute-start(bf16[512,512]{1,0:T(8,128)(2,1)S(1)} %collective-permute-done.11.refs_2_), channel_id=1, source_target_pairs={{0,8},{8,0},{16,24},{24,16},{32,40},{40,32},{48,56},{56,48},{64,72... | collective-permute-start | bytes 1572872 | tf_op jit(solution)/shard_map/ppermute | solution.py:29
  87.1 7.0 %collective-permute-start.7 = (bf16[512,512]{1,0:T(8,128)(2,1)S(1)}, bf16[512,512]{1,0:T(8,128)(2,1)S(1)}, u32[]{:S(2)}, u32[]{:S(2)}) collective-permute-start(bf16[512,512]{1,0:T(8,128)(2,1)S(1)} %shard_map.116.refs_0_), channel_id=1, source_target_pairs={{0,8},{8,0},{16,24},{24,16},{32,40},{40,32},{48,56},{56,48},{64,72... | collective-permute-start | bytes 1572872 | tf_op jit(solution)/shard_map/ppermute | solution.py:29
  89.1 5.2 %collective-permute-start.9 = (bf16[512,512]{1,0:T(8,128)(2,1)S(1)}, bf16[512,512]{1,0:T(8,128)(2,1)S(1)}, u32[]{:S(2)}, u32[]{:S(2)}) collective-permute-start(bf16[512,512]{1,0:T(8,128)(2,1)S(1)} %collective-permute-done.8.refs_2_), channel_id=1, source_target_pairs={{0,8},{8,0},{16,24},{24,16},{32,40},{40,32},{48,56},{56,48},{64,72... | collective-permute-start | bytes 1572872 | tf_op jit(solution)/shard_map/ppermute | solution.py:29

commit v4 on v3

--- a/solution.py
+++ b/solution.py
@@ -69,22 +69,24 @@
     )(first, second)
 
 
-def join_kernel(first, second, *refs):
-    out, rows = refs[-1], first.shape[0]
-    out[:rows, :] = first[...]
-    out[rows:, :] = second[...]
-
-
-def join(first, second, *ahead, flops=0):
-    rows, width = first.shape
+def join_kernel(parts, *refs):
+    out, first = refs[-1], 0
+    for part in refs[:parts]:
+        out[first : first + part.shape[0], :] = part[...]
+        first += part.shape[0]
+
+
+def join(parts, *ahead, flops=0):
+    rows = sum(part.shape[0] for part in parts)
+    width = parts[0].shape[1]
     return pl.pallas_call(
-        join_kernel,
-        out_shape=jax.ShapeDtypeStruct((2 * rows, width), first.dtype),
-        in_specs=[VMEM] * 2 + [ANY] * len(ahead),
+        functools.partial(join_kernel, len(parts)),
+        out_shape=jax.ShapeDtypeStruct((rows, width), parts[0].dtype),
+        in_specs=[VMEM] * len(parts) + [ANY] * len(ahead),
         out_specs=VMEM,
         compiler_params=pltpu.CompilerParams(vmem_limit_bytes=4 * 2**20),
         cost_estimate=pl.CostEstimate(flops=flops, bytes_accessed=4 * rows * width, transcendentals=0),
-    )(first, second, *ahead)
+    )(*parts, *ahead)
 
 
 def pick_kernel(chosen, params, local, momentum, ahead, spread, params_row, moment_row, held, sems):
@@ -122,7 +124,7 @@
         in_specs=[SMEM] + [ANY] * 4,
         out_specs=(VMEM,) * 3,
         scratch_shapes=[pltpu.VMEM((3, 8, length), jnp.float32), pltpu.SemaphoreType.DMA((3,))],
-        compiler_params=pltpu.CompilerParams(vmem_limit_bytes=60 * 2**20),
+        compiler_params=pltpu.CompilerParams(vmem_limit_bytes=4 * 2**20),
     )(fragment, params, local, momentum, ahead)
 
 
@@ -232,26 +234,28 @@
     spread, params_row, moment_row = pick(
         fragment, global_params, local_params[0], momentum, lax.axis_size("replica"), one
     )
+    everyone = lax.all_to_all(spread, "replica", 0, 0)
     next_one = along_z(one, 8)
-    everyone = lax.all_to_all(spread, "replica", 0, 0)
-    two = join(one, next_one, flops=10**10)
+    two = join((one, next_one), spread, flops=10**10)
     next_two = along_z(two, 4)
+    early = along_z(two, 2)
     global_next, momentum_next, inv = side(everyone, params_row, moment_row, block)
-    four = join(two, next_two, inv)
-    next_four = along_z(four, 2)
+    late = along_z(next_two, 2)
+    four = join((two, next_two), inv)
     four_y = across_y(four)
-    eight = join(four, next_four, flops=10**10)
+    next_four = join((early, late), flops=10**10)
     next_four_y = across_y(next_four)
+    eight = join((four, next_four))
     last = along_z(eight, 1)
     eight_c = across_core(eight)
-    eight_y = join(four_y, next_four_y)
+    eight_y = join((four_y, next_four_y))
     last_y = along_z(eight_y, 1)
     before = (0, 8, 4, 12, 2, 10, 6, 14)
-    after = tuple(moved + 1 for moved in before)
+    behind = tuple(moved + 1 for moved in before)
     count, features = block.shape
     width = own.shape[1]
     half = features // Y
-    layout = [(False, before), (True, before), (False, after), (True, after)]
+    layout = [(False, before), (True, before), (False, behind), (True, behind)]
     scratch = [pltpu.VMEM((half, width), jnp.bfloat16)]
     params = pltpu.CompilerParams(vmem_limit_bytes=8 * 2**20)
     flops = 2 * count * features * width

time: 97.3 us -> 94.6 us (0.972)
  waiting for transfers between devices: 13.9 us -> 7.65 us
  local copies, waits for them, and re-layouts: 0.03 us -> 3.14 us
  starting transfers between devices: 72.8 us -> 75.7 us
  Pallas kernels: 8.37 us -> 5.73 us
    ppermute x13 -> x14, waiting for transfers between devices: 13.9 us -> 7.65 us  [send(): lax.ppermute(array, 'fsdp', [(at(*here), at(*step(*here))) for here in so...]
    unnamed x10 -> x12, local copies, waits for them, and re-layouts: 0.03 us -> 3.14 us
    ppermute x13 -> x14, starting transfers between devices: 67.7 us -> 70.6 us  [send(): lax.ppermute(array, 'fsdp', [(at(*here), at(*step(*here))) for here in so...]
    pallas_call x1, Pallas kernels: 2.16 us -> 1.05 us  [pick(): pl.pallas_call(pick_kernel, out_shape=(jax.ShapeDtypeStruct((replicas, li...]
  transfers between devices with their start and end apart: 14 -> 15, of which waited for: 5 -> 5; matrix products, arithmetic and copies ran while one was open for 0% -> 0% of each run, Pallas kernels for 5% -> 4%
where the time goes in v4:
time: 94.6 us; the launch traced here: 93.8 us
  starting transfers between devices  75.7 us (80%)
  waiting for transfers between devices  7.65 us (8%)
  Pallas kernels  5.73 us (6%)
  local copies, waits for them, and re-layouts  3.14 us (3%)
  between operations  1.56 us (2%)
    ppermute x14, starting transfers between devices, send(): lax.ppermute(array, 'fsdp', [(at(*here), at(*step(*here))) for here in so...  70.6 us
    ppermute x14, waiting for transfers between devices, send(): lax.ppermute(array, 'fsdp', [(at(*here), at(*step(*here))) for here in so...  7.65 us
    all_to_all x1, starting transfers between devices, shards(): everyone = lax.all_to_all(spread, 'replica', 0, 0)  5.04 us
    unnamed x12, local copies, waits for them, and re-layouts  3.14 us
    pallas_call x1, Pallas kernels, shards(): pl.pallas_call(functools.partial(other_kernel, rows, layout), out_shape=(...  2.42 us
  transfers between devices with their start and end apart: 15, of which 5 were waited for; matrix products, arithmetic and copies ran while one was open for 0% of the time, Pallas kernels for 4%

profile of v4, /device:TPU:1, one launch (start us, length us, event | category | flops | bytes accessed | tf_op | source)
XLA Modules:
  0.0 93.8 jit_solution(6613481928823480844)
XLA Ops:
  0.6 19.2 %collective-permute-start.1 = (bf16[32,512]{1,0:T(8,128)(2,1)}, bf16[32,512]{1,0:T(8,128)(2,1)S(1)}, u32[]{:S(2)}, u32[]{:S(2)}) collective-permute-start(bf16[32,512]{1,0:T(8,128)(2,1)} %bitcast.16), channel_id=1, source_target_pairs={{0,0},{8,504},{16,16},{24,8},{32,32},{40,24},{48,48},{56,40},{64,6... | collective-permute-start | bytes 98312 | tf_op jit(solution)/shard_map/ppermute | solution.py:29
  19.9 0.0 collective-permute-start
  19.9 1.3 %collective-permute-done.1.second = bf16[32,512]{1,0:T(8,128)(2,1)S(1)} collective-permute-done((bf16[32,512]{1,0:T(8,128)(2,1)}, bf16[32,512]{1,0:T(8,128)(2,1)S(1)}, u32[]{:S(2)}, u32[]{:S(2)}) %collective-permute-start.1) | collective-permute-done | bytes 32800 | tf_op jit(solution)/shard_map/ppermute | solution.py:29
  21.2 2.2 %collective-permute-done.first = bf16[32,512]{1,0:T(8,128)(2,1)S(1)} collective-permute-done((bf16[32,512]{1,0:T(8,128)(2,1)}, bf16[32,512]{1,0:T(8,128)(2,1)S(1)}, u32[]{:S(2)}, u32[]{:S(2)}) %collective-permute-start) | collective-permute-done | bytes 32800 | tf_op jit(solution)/shard_map/ppermute | solution.py:29
  23.4 8.2 %collective-permute-start.2 = (bf16[64,512]{1,0:T(8,128)(2,1)S(1)}, bf16[64,512]{1,0:T(8,128)(2,1)S(1)}, u32[]{:S(2)}, u32[]{:S(2)}) collective-permute-start(bf16[64,512]{1,0:T(8,128)(2,1)S(1)} %shard_map.111.ahead.refs_0_), channel_id=1, source_target_pairs={{0,128},{8,392},{16,144},{24,408},{32,160},{40,424},{48,176},{56,4... | collective-permute-start | bytes 196616 | tf_op jit(solution)/shard_map/ppermute | solution.py:29
  32.2 0.0 copy-start.2
  32.3 1.0 %copy-done.2 = f32[16,8192]{1,0:T(8,128)S(1)} copy-done((f32[16,8192]{1,0:T(8,128)S(1)}, f32[16,8192]{1,0:T(8,128)}, u32[]{:S(2)}) %copy-start.2) | copy-done | bytes 524312
  33.3 0.0 copy-start.3
  33.3 1.0 %copy-done.3 = f32[1,16,8192]{2,1,0:T(8,128)S(1)} copy-done((f32[1,16,8192]{2,1,0:T(8,128)S(1)}, f32[1,16,8192]{2,1,0:T(8,128)}, u32[]{:S(2)}) %copy-start.3) | copy-done | bytes 524312
  34.3 0.0 copy-start.4
  34.3 1.0 %copy-done.4 = f32[16,8192]{1,0:T(8,128)S(1)} copy-done((f32[16,8192]{1,0:T(8,128)S(1)}, f32[16,8192]{1,0:T(8,128)}, u32[]{:S(2)}) %copy-start.4) | copy-done | bytes 524312
  35.4 1.1 %shard_map.112 = (f32[8,64,128]{2,1,0:T(8,128)}, f32[64,128]{1,0:T(8,128)S(1)}, f32[64,128]{1,0:T(8,128)S(1)}) custom-call(s32[1]{0:T(128)S(6)} %copy.12.chosen, f32[16,8192]{1,0:T(8,128)S(1)} %copy-done.2, f32[16,8192]{1,0:T(8,128)S(1)} %bitcast.13, f32[16,8192]{1,0:T(8,128)S(1)} %copy-done.4, bf16[64,512]{1,0:T(8,128)(2,1)S(1)} %shard_map.111.ahead.refs_0_), custom_call_target="tpu_custom_call" | custom-call | tf_op jit(solution)/shard_map/pallas_call | solution.py:121
  36.4 1.0 %collective-permute-done.2.refs_1_ = bf16[64,512]{1,0:T(8,128)(2,1)S(1)} collective-permute-done((bf16[64,512]{1,0:T(8,128)(2,1)S(1)}, bf16[64,512]{1,0:T(8,128)(2,1)S(1)}, u32[]{:S(2)}, u32[]{:S(2)}) %collective-permute-start.2) | collective-permute-done | bytes 65568 | tf_op jit(solution)/shard_map/ppermute | solution.py:29
  37.4 0.0 copy-start
  37.5 6.0 %collective-permute-start.3 = (bf16[128,512]{1,0:T(8,128)(2,1)S(1)}, bf16[128,512]{1,0:T(8,128)(2,1)S(1)}, u32[]{:S(2)}, u32[]{:S(2)}) collective-permute-start(bf16[128,512]{1,0:T(8,128)(2,1)S(1)} %shard_map.113.refs_0_), channel_id=1, source_target_pairs={{0,64},{8,456},{16,80},{24,472},{32,96},{40,488},{48,112},{56,504}... | collective-permute-start | bytes 393224 | tf_op jit(solution)/shard_map/ppermute | solution.py:29
  43.4 5.0 %all-to-all-start = ((f32[8,64,128]{2,1,0:T(8,128)}), f32[8,64,128]{2,1,0:T(8,128)S(1)}, u32[]{:S(2)}, u32[]{:S(2)}) async-start(f32[8,64,128]{2,1,0:T(8,128)} %get-tuple-element.14.refs_2_), calls=%async_computation | async-start | bytes 524288 | tf_op jit(solution)/shard_map/all_to_all | solution.py:237
  48.5 2.5 %collective-permute-start.5 = (bf16[128,512]{1,0:T(8,128)(2,1)S(1)}, bf16[128,512]{1,0:T(8,128)(2,1)S(1)}, u32[]{:S(2)}, u32[]{:S(2)}) collective-permute-start(bf16[128,512]{1,0:T(8,128)(2,1)S(1)} %shard_map.113.refs_0_), channel_id=1, source_target_pairs={{0,32},{8,488},{16,48},{24,504},{32,64},{40,8},{48,80},{56,24},{64... | collective-permute-start | bytes 393224 | tf_op jit(solution)/shard_map/ppermute | solution.py:29
  51.0 0.0 collective-permute-done.3.refs_1_
  51.0 7.5 %collective-permute-start.6 = (bf16[128,512]{1,0:T(8,128)(2,1)S(1)}, bf16[128,512]{1,0:T(8,128)(2,1)S(1)}, u32[]{:S(2)}, u32[]{:S(2)}) collective-permute-start(bf16[128,512]{1,0:T(8,128)(2,1)S(1)} %collective-permute-done.3.refs_1_), channel_id=1, source_target_pairs={{0,32},{8,488},{16,48},{24,504},{32,64},{40,8},{48,80},{56,24},{64... | collective-permute-start | bytes 393224 | tf_op jit(solution)/shard_map/ppermute | solution.py:29
  58.5 0.0 all-to-all-done.everyone
  58.5 0.0 copy-done
  58.5 0.8 shard_map.114
  59.3 4.5 %collective-permute-start.4 = (bf16[256,512]{1,0:T(8,128)(2,1)S(1)}, bf16[256,512]{1,0:T(8,128)(2,1)S(1)}, u32[]{:S(2)}, u32[]{:S(2)}) collective-permute-start(bf16[256,512]{1,0:T(8,128)(2,1)S(1)} %shard_map.115.refs_0_), channel_id=1, source_target_pairs={{0,512},{8,520},{16,528},{24,536},{32,544},{40,552},{48,560},{56,5... | collective-permute-start | bytes 786440 | tf_op jit(solution)/shard_map/ppermute | solution.py:29
  63.9 0.0 collective-permute-done.5.refs_0_
  63.9 0.0 collective-permute-done.6.refs_1_
  63.9 2.3 %collective-permute-start.7 = (bf16[256,512]{1,0:T(8,128)(2,1)S(1)}, bf16[256,512]{1,0:T(8,128)(2,1)S(1)}, u32[]{:S(2)}, u32[]{:S(2)}) collective-permute-start(bf16[256,512]{1,0:T(8,128)(2,1)S(1)} %shard_map.116.refs_1_), channel_id=1, source_target_pairs={{0,512},{8,520},{16,528},{24,536},{32,544},{40,552},{48,560},{56,5... | collective-permute-start | bytes 786440 | tf_op jit(solution)/shard_map/ppermute | solution.py:29
  66.2 0.0 copy-start.1
  66.3 0.0 copy-start.5
  66.3 4.6 %collective-permute-start.12 = (bf16[512,512]{1,0:T(8,128)(2,1)S(1)}, bf16[512,512]{1,0:T(8,128)(2,1)S(1)}, u32[]{:S(2)}, u32[]{:S(2)}) collective-permute-start(bf16[512,512]{1,0:T(8,128)(2,1)S(1)} %shard_map.118.refs_0_), channel_id=1, source_target_pairs={{0,16},{8,504},{16,32},{24,8},{32,48},{40,24},{48,64},{56,40},{64,... | collective-permute-start | bytes 1572872 | tf_op jit(solution)/shard_map/ppermute | solution.py:29
  70.8 0.0 collective-permute-done.4.refs_0_
  70.8 2.9 %collective-permute-done.7.refs_1_ = bf16[256,512]{1,0:T(8,128)(2,1)S(1)} collective-permute-done((bf16[256,512]{1,0:T(8,128)(2,1)S(1)}, bf16[256,512]{1,0:T(8,128)(2,1)S(1)}, u32[]{:S(2)}, u32[]{:S(2)}) %collective-permute-start.7) | collective-permute-done | bytes 262176 | tf_op jit(solution)/shard_map/ppermute | solution.py:29
  73.8 6.4 %collective-permute-start.9 = (bf16[512,512]{1,0:T(8,128)(2,1)S(1)}, bf16[512,512]{1,0:T(8,128)(2,1)S(1)}, u32[]{:S(2)}, u32[]{:S(2)}) collective-permute-start(bf16[512,512]{1,0:T(8,128)(2,1)S(1)} %shard_map.117.refs_0_), channel_id=1, source_target_pairs={{0,16},{8,504},{16,32},{24,8},{32,48},{40,24},{48,64},{56,40},{64,... | collective-permute-start | bytes 1572872 | tf_op jit(solution)/shard_map/ppermute | solution.py:29
  80.2 1.9 %collective-permute-start.11 = (bf16[512,512]{1,0:T(8,128)(2,1)S(1)}, bf16[512,512]{1,0:T(8,128)(2,1)S(1)}, u32[]{:S(2)}, u32[]{:S(2)}) collective-permute-start(bf16[512,512]{1,0:T(8,128)(2,1)S(1)} %shard_map.118.refs_0_), channel_id=1, source_target_pairs={{0,8},{8,0},{16,24},{24,16},{32,40},{40,32},{48,56},{56,48},{64,72... | collective-permute-start | bytes 1572872 | tf_op jit(solution)/shard_map/ppermute | solution.py:29
  82.1 0.0 collective-permute-done.12.refs_2_
  82.1 2.4 %collective-permute-start.13 = (bf16[512,512]{1,0:T(8,128)(2,1)S(1)}, bf16[512,512]{1,0:T(8,128)(2,1)S(1)}, u32[]{:S(2)}, u32[]{:S(2)}) collective-permute-start(bf16[512,512]{1,0:T(8,128)(2,1)S(1)} %collective-permute-done.12.refs_2_), channel_id=1, source_target_pairs={{0,8},{8,0},{16,24},{24,16},{32,40},{40,32},{48,56},{56,48},{64,72... | collective-permute-start | bytes 1572872 | tf_op jit(solution)/shard_map/ppermute | solution.py:29
  84.6 1.9 %collective-permute-start.8 = (bf16[512,512]{1,0:T(8,128)(2,1)S(1)}, bf16[512,512]{1,0:T(8,128)(2,1)S(1)}, u32[]{:S(2)}, u32[]{:S(2)}) collective-permute-start(bf16[512,512]{1,0:T(8,128)(2,1)S(1)} %shard_map.117.refs_0_), channel_id=1, source_target_pairs={{0,8},{8,0},{16,24},{24,16},{32,40},{40,32},{48,56},{56,48},{64,72... | collective-permute-start | bytes 1572872 | tf_op jit(solution)/shard_map/ppermute | solution.py:29
  86.5 0.0 collective-permute-done.9.refs_2_
  86.5 3.3 %collective-permute-start.10 = (bf16[512,512]{1,0:T(8,128)(2,1)S(1)}, bf16[512,512]{1,0:T(8,128)(2,1)S(1)}, u32[]{:S(2)}, u32[]{:S(2)}) collective-permute-start(bf16[512,512]{1,0:T(8,128)(2,1)S(1)} %collective-permute-done.9.refs_2_), channel_id=1, source_target_pairs={{0,8},{8,0},{16,24},{24,16},{32,40},{40,32},{48,56},{56,48},{64,72... | collective-permute-start | bytes 1572872 | tf_op jit(solution)/shard_map/ppermute | solution.py:29
  89.8 0.0 collective-permute-done.11.refs_1_
  89.8 0.0 collective-permute-done.13.refs_3_
  89.9 0.0 copy-done.1
  89.9 0.0 copy-done.5
  89.9 1.3 %shard_map.119 = (f32[128,512]{1,0:T(8,128)S(1)}, f32[128,2048]{1,0:T(8,128)S(1)}) custom-call(bf16[512,512]{1,0:T(8,128)(2,1)S(1)} %shard_map.118.refs_0_, bf16[512,512]{1,0:T(8,128)(2,1)S(1)} %collective-permute-done.11.refs_1_, bf16[512,512]{1,0:T(8,128)(2,1)S(1)} %collective-permute-done.12.refs_2_, ...), custom_call_target="tpu_custom_call" | custom-call | flops 536870912 | bytes 4194304 | tf_op jit(solution)/shard_map/pallas_call | solution.py:263
  91.2 0.0 collective-permute-done.8.refs_1_
  91.2 0.2 collective-permute-done.10.refs_3_
  91.4 2.4 %shard_map.120 = (bf16[128,512]{1,0:T(8,128)(2,1)}, bf16[128,4096]{1,0:T(8,128)(2,1)}) custom-call(bf16[512,512]{1,0:T(8,128)(2,1)S(1)} %shard_map.117.refs_0_, bf16[512,512]{1,0:T(8,128)(2,1)S(1)} %collective-permute-done.8.refs_1_, bf16[512,512]{1,0:T(8,128)(2,1)S(1)} %collective-permute-done.9.refs_2_, ...), custom_call_target="tpu_custom_call" | custom-call | flops 536870912 | bytes 4194304 | tf_op jit(solution)/shard_map/pallas_call | solution.py:275
  (6 shorter events, 0.1 us)
Async XLA Ops:
  0.6 20.6 %collective-permute-start.1 = (bf16[32,512]{1,0:T(8,128)(2,1)}, bf16[32,512]{1,0:T(8,128)(2,1)S(1)}, u32[]{:S(2)}, u32[]{:S(2)}) collective-permute-start(bf16[32,512]{1,0:T(8,128)(2,1)} %bitcast.16), channel_id=1, source_target_pairs={{0,0},{8,504},{16,16},{24,8},{32,32},{40,24},{48,48},{56,40},{64,6... | collective-permute-start | bytes 98312 | tf_op jit(solution)/shard_map/ppermute | solution.py:29
  19.9 3.6 %collective-permute-start = (bf16[32,512]{1,0:T(8,128)(2,1)}, bf16[32,512]{1,0:T(8,128)(2,1)S(1)}, u32[]{:S(2)}, u32[]{:S(2)}) collective-permute-start(bf16[32,512]{1,0:T(8,128)(2,1)} %bitcast.17), channel_id=1, source_target_pairs={{0,504},{8,0},{16,8},{24,16},{32,24},{40,32},{48,40},{56,48},{64,5... | collective-permute-start | bytes 98312 | tf_op jit(solution)/shard_map/ppermute | solution.py:29
  23.4 14.0 %collective-permute-start.2 = (bf16[64,512]{1,0:T(8,128)(2,1)S(1)}, bf16[64,512]{1,0:T(8,128)(2,1)S(1)}, u32[]{:S(2)}, u32[]{:S(2)}) collective-permute-start(bf16[64,512]{1,0:T(8,128)(2,1)S(1)} %shard_map.111.ahead.refs_0_), channel_id=1, source_target_pairs={{0,128},{8,392},{16,144},{24,408},{32,160},{40,424},{48,176},{56,4... | collective-permute-start | bytes 196616 | tf_op jit(solution)/shard_map/ppermute | solution.py:29
  32.2 1.0 %copy-start.2 = (f32[16,8192]{1,0:T(8,128)S(1)}, f32[16,8192]{1,0:T(8,128)}, u32[]{:S(2)}) copy-start(f32[16,8192]{1,0:T(8,128)} %params.1) | copy-start | bytes 1572868
  33.3 1.0 %copy-start.3 = (f32[1,16,8192]{2,1,0:T(8,128)S(1)}, f32[1,16,8192]{2,1,0:T(8,128)}, u32[]{:S(2)}) copy-start(f32[1,16,8192]{2,1,0:T(8,128)} %param.13) | copy-start | bytes 1572868
  34.3 1.0 %copy-start.4 = (f32[16,8192]{1,0:T(8,128)S(1)}, f32[16,8192]{1,0:T(8,128)}, u32[]{:S(2)}) copy-start(f32[16,8192]{1,0:T(8,128)} %momentum.1) | copy-start | bytes 1572868
  37.4 21.0 %copy-start = (bf16[1,128,4096]{2,1,0:T(8,128)(2,1)S(1)}, bf16[1,128,4096]{2,1,0:T(8,128)(2,1)}, u32[]{:S(2)}) copy-start(bf16[1,128,4096]{2,1,0:T(8,128)(2,1)} %param.8) | copy-start | bytes 3145732
  37.5 13.5 %collective-permute-start.3 = (bf16[128,512]{1,0:T(8,128)(2,1)S(1)}, bf16[128,512]{1,0:T(8,128)(2,1)S(1)}, u32[]{:S(2)}, u32[]{:S(2)}) collective-permute-start(bf16[128,512]{1,0:T(8,128)(2,1)S(1)} %shard_map.113.refs_0_), channel_id=1, source_target_pairs={{0,64},{8,456},{16,80},{24,472},{32,96},{40,488},{48,112},{56,504}... | collective-permute-start | bytes 393224 | tf_op jit(solution)/shard_map/ppermute | solution.py:29
  43.4 15.0 %all-to-all-start = ((f32[8,64,128]{2,1,0:T(8,128)}), f32[8,64,128]{2,1,0:T(8,128)S(1)}, u32[]{:S(2)}, u32[]{:S(2)}) async-start(f32[8,64,128]{2,1,0:T(8,128)} %get-tuple-element.14.refs_2_), calls=%async_computation | async-start | bytes 524288 | tf_op jit(solution)/shard_map/all_to_all | solution.py:237
  48.5 15.4 %collective-permute-start.5 = (bf16[128,512]{1,0:T(8,128)(2,1)S(1)}, bf16[128,512]{1,0:T(8,128)(2,1)S(1)}, u32[]{:S(2)}, u32[]{:S(2)}) collective-permute-start(bf16[128,512]{1,0:T(8,128)(2,1)S(1)} %shard_map.113.refs_0_), channel_id=1, source_target_pairs={{0,32},{8,488},{16,48},{24,504},{32,64},{40,8},{48,80},{56,24},{64... | collective-permute-start | bytes 393224 | tf_op jit(solution)/shard_map/ppermute | solution.py:29
  51.0 12.9 %collective-permute-start.6 = (bf16[128,512]{1,0:T(8,128)(2,1)S(1)}, bf16[128,512]{1,0:T(8,128)(2,1)S(1)}, u32[]{:S(2)}, u32[]{:S(2)}) collective-permute-start(bf16[128,512]{1,0:T(8,128)(2,1)S(1)} %collective-permute-done.3.refs_1_), channel_id=1, source_target_pairs={{0,32},{8,488},{16,48},{24,504},{32,64},{40,8},{48,80},{56,24},{64... | collective-permute-start | bytes 393224 | tf_op jit(solution)/shard_map/ppermute | solution.py:29
  59.3 11.5 %collective-permute-start.4 = (bf16[256,512]{1,0:T(8,128)(2,1)S(1)}, bf16[256,512]{1,0:T(8,128)(2,1)S(1)}, u32[]{:S(2)}, u32[]{:S(2)}) collective-permute-start(bf16[256,512]{1,0:T(8,128)(2,1)S(1)} %shard_map.115.refs_0_), channel_id=1, source_target_pairs={{0,512},{8,520},{16,528},{24,536},{32,544},{40,552},{48,560},{56,5... | collective-permute-start | bytes 786440 | tf_op jit(solution)/shard_map/ppermute | solution.py:29
  63.9 9.8 %collective-permute-start.7 = (bf16[256,512]{1,0:T(8,128)(2,1)S(1)}, bf16[256,512]{1,0:T(8,128)(2,1)S(1)}, u32[]{:S(2)}, u32[]{:S(2)}) collective-permute-start(bf16[256,512]{1,0:T(8,128)(2,1)S(1)} %shard_map.116.refs_1_), channel_id=1, source_target_pairs={{0,512},{8,520},{16,528},{24,536},{32,544},{40,552},{48,560},{56,5... | collective-permute-start | bytes 786440 | tf_op jit(solution)/shard_map/ppermute | solution.py:29
  66.2 23.6 %copy-start.1 = (bf16[1,128,512]{2,1,0:T(8,128)(2,1)S(1)}, bf16[1,128,512]{2,1,0:T(8,128)(2,1)}, u32[]{:S(2)}) copy-start(bf16[1,128,512]{2,1,0:T(8,128)(2,1)} %param.11) | copy-start | bytes 393220
  66.3 23.6 %copy-start.5 = (bf16[1,4096]{1,0:T(2,128)(2,1)S(1)}, bf16[1,4096]{1,0:T(2,128)(2,1)}, u32[]{:S(2)}) copy-start(bf16[1,4096]{1,0:T(2,128)(2,1)} %refs_6_.3) | copy-start | bytes 24580
  66.3 15.9 %collective-permute-start.12 = (bf16[512,512]{1,0:T(8,128)(2,1)S(1)}, bf16[512,512]{1,0:T(8,128)(2,1)S(1)}, u32[]{:S(2)}, u32[]{:S(2)}) collective-permute-start(bf16[512,512]{1,0:T(8,128)(2,1)S(1)} %shard_map.118.refs_0_), channel_id=1, source_target_pairs={{0,16},{8,504},{16,32},{24,8},{32,48},{40,24},{48,64},{56,40},{64,... | collective-permute-start | bytes 1572872 | tf_op jit(solution)/shard_map/ppermute | solution.py:29
  73.8 12.7 %collective-permute-start.9 = (bf16[512,512]{1,0:T(8,128)(2,1)S(1)}, bf16[512,512]{1,0:T(8,128)(2,1)S(1)}, u32[]{:S(2)}, u32[]{:S(2)}) collective-permute-start(bf16[512,512]{1,0:T(8,128)(2,1)S(1)} %shard_map.117.refs_0_), channel_id=1, source_target_pairs={{0,16},{8,504},{16,32},{24,8},{32,48},{40,24},{48,64},{56,40},{64,... | collective-permute-start | bytes 1572872 | tf_op jit(solution)/shard_map/ppermute | solution.py:29
  80.2 9.6 %collective-permute-start.11 = (bf16[512,512]{1,0:T(8,128)(2,1)S(1)}, bf16[512,512]{1,0:T(8,128)(2,1)S(1)}, u32[]{:S(2)}, u32[]{:S(2)}) collective-permute-start(bf16[512,512]{1,0:T(8,128)(2,1)S(1)} %shard_map.118.refs_0_), channel_id=1, source_target_pairs={{0,8},{8,0},{16,24},{24,16},{32,40},{40,32},{48,56},{56,48},{64,72... | collective-permute-start | bytes 1572872 | tf_op jit(solution)/shard_map/ppermute | solution.py:29
  82.1 7.7 %collective-permute-start.13 = (bf16[512,512]{1,0:T(8,128)(2,1)S(1)}, bf16[512,512]{1,0:T(8,128)(2,1)S(1)}, u32[]{:S(2)}, u32[]{:S(2)}) collective-permute-start(bf16[512,512]{1,0:T(8,128)(2,1)S(1)} %collective-permute-done.12.refs_2_), channel_id=1, source_target_pairs={{0,8},{8,0},{16,24},{24,16},{32,40},{40,32},{48,56},{56,48},{64,72... | collective-permute-start | bytes 1572872 | tf_op jit(solution)/shard_map/ppermute | solution.py:29
  84.6 6.6 %collective-permute-start.8 = (bf16[512,512]{1,0:T(8,128)(2,1)S(1)}, bf16[512,512]{1,0:T(8,128)(2,1)S(1)}, u32[]{:S(2)}, u32[]{:S(2)}) collective-permute-start(bf16[512,512]{1,0:T(8,128)(2,1)S(1)} %shard_map.117.refs_0_), channel_id=1, source_target_pairs={{0,8},{8,0},{16,24},{24,16},{32,40},{40,32},{48,56},{56,48},{64,72... | collective-permute-start | bytes 1572872 | tf_op jit(solution)/shard_map/ppermute | solution.py:29
  86.5 4.9 %collective-permute-start.10 = (bf16[512,512]{1,0:T(8,128)(2,1)S(1)}, bf16[512,512]{1,0:T(8,128)(2,1)S(1)}, u32[]{:S(2)}, u32[]{:S(2)}) collective-permute-start(bf16[512,512]{1,0:T(8,128)(2,1)S(1)} %collective-permute-done.9.refs_2_), channel_id=1, source_target_pairs={{0,8},{8,0},{16,24},{24,16},{32,40},{40,32},{48,56},{56,48},{64,72... | collective-permute-start | bytes 1572872 | tf_op jit(solution)/shard_map/ppermute | solution.py:29

commit v5 on v4

--- a/solution.py
+++ b/solution.py
@@ -207,7 +207,7 @@
 
 def other_kernel(rows, layout, *refs):
     pieces = refs[: len(layout)]
-    tokens, inv, gain, upstream, partial, gained, projected, token_grad, full = refs[len(layout) :]
+    tokens, inv, gain, upstream, partial, gained, projected, token_grad, full, made, sems = refs[len(layout) :]
     for piece, (other_core, offsets) in zip(pieces, layout):
         put(piece, full, rows, other_core, offsets)
     y, _, _ = position()
@@ -219,11 +219,17 @@
     def finish(column, first, values):
         lanes = lanes_of(column, full.shape[0], first, CHUNK)
         unit = tokens[:, lanes].astype(jnp.float32) * inv[...]
-        token_grad[:, lanes] = (inv[...] * (values - unit * inner)).astype(jnp.bfloat16)
-
+        made[:, lanes] = (inv[...] * (values - unit * inner)).astype(jnp.bfloat16)
+        copy = pltpu.make_async_copy(made.at[:, lanes], token_grad.at[:, lanes], sems.at[len(copies)])
+        copy.start()
+        copies.append(copy)
+
+    copies = []
     for first in range(0, full.shape[0], CHUNK):
+        finish(y, first, gained[:, first : first + CHUNK])
         finish(1 - y, first, gained_of(above, gain, full, 1 - y, first))
-        finish(y, first, gained[:, first : first + CHUNK])
+    for copy in copies:
+        copy.wait()
 
 
 def shards(tokens, norm_gain, weight, cotangent, global_params, local_params, momentum, fragment):
@@ -279,8 +285,12 @@
             jax.ShapeDtypeStruct((count, features), jnp.bfloat16),
         ),
         in_specs=[VMEM] * (len(layout) + 6),
-        out_specs=(VMEM, VMEM),
-        scratch_shapes=scratch,
+        out_specs=(VMEM, ANY),
+        scratch_shapes=[
+            *scratch,
+            pltpu.VMEM((count, features), jnp.bfloat16),
+            pltpu.SemaphoreType.DMA((features // CHUNK,)),
+        ],
         compiler_params=params,
         cost_estimate=cost,
     )(

time: 94.6 us -> 94.9 us (level)
  transfers between devices with their start and end apart: 15 -> 15, of which waited for: 5 -> 5; matrix products, arithmetic and copies ran while one was open for 0% -> 0% of each run, Pallas kernels for 4% -> 3%
where the time goes in v5:
time: 94.9 us; the launch traced here: 94.2 us
  starting transfers between devices  75.7 us (80%)
  waiting for transfers between devices  7.65 us (8%)
  Pallas kernels  6.11 us (6%)
  local copies, waits for them, and re-layouts  3.14 us (3%)
  between operations  1.56 us (2%)
    ppermute x14, starting transfers between devices, send(): lax.ppermute(array, 'fsdp', [(at(*here), at(*step(*here))) for here in so...  70.6 us
    ppermute x14, waiting for transfers between devices, send(): lax.ppermute(array, 'fsdp', [(at(*here), at(*step(*here))) for here in so...  7.65 us
    all_to_all x1, starting transfers between devices, shards(): everyone = lax.all_to_all(spread, 'replica', 0, 0)  5.04 us
    unnamed x12, local copies, waits for them, and re-layouts  3.14 us
    pallas_call x1, Pallas kernels, shards(): pl.pallas_call(functools.partial(other_kernel, rows, layout), out_shape=(...  2.8 us
  transfers between devices with their start and end apart: 15, of which 5 were waited for; matrix products, arithmetic and copies ran while one was open for 0% of the time, Pallas kernels for 3%

profile of v5, /device:TPU:1, one launch (start us, length us, event | category | flops | bytes accessed | tf_op | source)
XLA Modules:
  0.0 94.2 jit_solution(16153584184515662499)
XLA Ops:
  0.6 19.2 %collective-permute-start.1 = (bf16[32,512]{1,0:T(8,128)(2,1)}, bf16[32,512]{1,0:T(8,128)(2,1)S(1)}, u32[]{:S(2)}, u32[]{:S(2)}) collective-permute-start(bf16[32,512]{1,0:T(8,128)(2,1)} %bitcast.16), channel_id=1, source_target_pairs={{0,0},{8,504},{16,16},{24,8},{32,32},{40,24},{48,48},{56,40},{64,6... | collective-permute-start | bytes 98312 | tf_op jit(solution)/shard_map/ppermute | solution.py:29
  19.9 0.0 collective-permute-start
  19.9 1.3 %collective-permute-done.1.second = bf16[32,512]{1,0:T(8,128)(2,1)S(1)} collective-permute-done((bf16[32,512]{1,0:T(8,128)(2,1)}, bf16[32,512]{1,0:T(8,128)(2,1)S(1)}, u32[]{:S(2)}, u32[]{:S(2)}) %collective-permute-start.1) | collective-permute-done | bytes 32800 | tf_op jit(solution)/shard_map/ppermute | solution.py:29
  21.2 2.2 %collective-permute-done.first = bf16[32,512]{1,0:T(8,128)(2,1)S(1)} collective-permute-done((bf16[32,512]{1,0:T(8,128)(2,1)}, bf16[32,512]{1,0:T(8,128)(2,1)S(1)}, u32[]{:S(2)}, u32[]{:S(2)}) %collective-permute-start) | collective-permute-done | bytes 32800 | tf_op jit(solution)/shard_map/ppermute | solution.py:29
  23.4 8.2 %collective-permute-start.2 = (bf16[64,512]{1,0:T(8,128)(2,1)S(1)}, bf16[64,512]{1,0:T(8,128)(2,1)S(1)}, u32[]{:S(2)}, u32[]{:S(2)}) collective-permute-start(bf16[64,512]{1,0:T(8,128)(2,1)S(1)} %shard_map.111.ahead.refs_0_), channel_id=1, source_target_pairs={{0,128},{8,392},{16,144},{24,408},{32,160},{40,424},{48,176},{56,4... | collective-permute-start | bytes 196616 | tf_op jit(solution)/shard_map/ppermute | solution.py:29
  32.2 0.0 copy-start.2
  32.3 1.0 %copy-done.2 = f32[16,8192]{1,0:T(8,128)S(1)} copy-done((f32[16,8192]{1,0:T(8,128)S(1)}, f32[16,8192]{1,0:T(8,128)}, u32[]{:S(2)}) %copy-start.2) | copy-done | bytes 524312
  33.3 0.0 copy-start.3
  33.3 1.0 %copy-done.3 = f32[1,16,8192]{2,1,0:T(8,128)S(1)} copy-done((f32[1,16,8192]{2,1,0:T(8,128)S(1)}, f32[1,16,8192]{2,1,0:T(8,128)}, u32[]{:S(2)}) %copy-start.3) | copy-done | bytes 524312
  34.3 0.0 copy-start.4
  34.3 1.0 %copy-done.4 = f32[16,8192]{1,0:T(8,128)S(1)} copy-done((f32[16,8192]{1,0:T(8,128)S(1)}, f32[16,8192]{1,0:T(8,128)}, u32[]{:S(2)}) %copy-start.4) | copy-done | bytes 524312
  35.4 1.1 %shard_map.112 = (f32[8,64,128]{2,1,0:T(8,128)}, f32[64,128]{1,0:T(8,128)S(1)}, f32[64,128]{1,0:T(8,128)S(1)}) custom-call(s32[1]{0:T(128)S(6)} %copy.12.chosen, f32[16,8192]{1,0:T(8,128)S(1)} %copy-done.2, f32[16,8192]{1,0:T(8,128)S(1)} %bitcast.13, f32[16,8192]{1,0:T(8,128)S(1)} %copy-done.4, bf16[64,512]{1,0:T(8,128)(2,1)S(1)} %shard_map.111.ahead.refs_0_), custom_call_target="tpu_custom_call" | custom-call | tf_op jit(solution)/shard_map/pallas_call | solution.py:121
  36.4 1.0 %collective-permute-done.2.refs_1_ = bf16[64,512]{1,0:T(8,128)(2,1)S(1)} collective-permute-done((bf16[64,512]{1,0:T(8,128)(2,1)S(1)}, bf16[64,512]{1,0:T(8,128)(2,1)S(1)}, u32[]{:S(2)}, u32[]{:S(2)}) %collective-permute-start.2) | collective-permute-done | bytes 65568 | tf_op jit(solution)/shard_map/ppermute | solution.py:29
  37.4 0.0 copy-start
  37.5 6.0 %collective-permute-start.3 = (bf16[128,512]{1,0:T(8,128)(2,1)S(1)}, bf16[128,512]{1,0:T(8,128)(2,1)S(1)}, u32[]{:S(2)}, u32[]{:S(2)}) collective-permute-start(bf16[128,512]{1,0:T(8,128)(2,1)S(1)} %shard_map.113.refs_0_), channel_id=1, source_target_pairs={{0,64},{8,456},{16,80},{24,472},{32,96},{40,488},{48,112},{56,504}... | collective-permute-start | bytes 393224 | tf_op jit(solution)/shard_map/ppermute | solution.py:29
  43.4 5.0 %all-to-all-start = ((f32[8,64,128]{2,1,0:T(8,128)}), f32[8,64,128]{2,1,0:T(8,128)S(1)}, u32[]{:S(2)}, u32[]{:S(2)}) async-start(f32[8,64,128]{2,1,0:T(8,128)} %get-tuple-element.14.refs_2_), calls=%async_computation | async-start | bytes 524288 | tf_op jit(solution)/shard_map/all_to_all | solution.py:243
  48.5 2.5 %collective-permute-start.5 = (bf16[128,512]{1,0:T(8,128)(2,1)S(1)}, bf16[128,512]{1,0:T(8,128)(2,1)S(1)}, u32[]{:S(2)}, u32[]{:S(2)}) collective-permute-start(bf16[128,512]{1,0:T(8,128)(2,1)S(1)} %shard_map.113.refs_0_), channel_id=1, source_target_pairs={{0,32},{8,488},{16,48},{24,504},{32,64},{40,8},{48,80},{56,24},{64... | collective-permute-start | bytes 393224 | tf_op jit(solution)/shard_map/ppermute | solution.py:29
  51.0 0.0 collective-permute-done.3.refs_1_
  51.0 7.5 %collective-permute-start.6 = (bf16[128,512]{1,0:T(8,128)(2,1)S(1)}, bf16[128,512]{1,0:T(8,128)(2,1)S(1)}, u32[]{:S(2)}, u32[]{:S(2)}) collective-permute-start(bf16[128,512]{1,0:T(8,128)(2,1)S(1)} %collective-permute-done.3.refs_1_), channel_id=1, source_target_pairs={{0,32},{8,488},{16,48},{24,504},{32,64},{40,8},{48,80},{56,24},{64... | collective-permute-start | bytes 393224 | tf_op jit(solution)/shard_map/ppermute | solution.py:29
  58.5 0.0 all-to-all-done.everyone
  58.5 0.0 copy-done
  58.5 0.8 shard_map.114
  59.3 4.5 %collective-permute-start.4 = (bf16[256,512]{1,0:T(8,128)(2,1)S(1)}, bf16[256,512]{1,0:T(8,128)(2,1)S(1)}, u32[]{:S(2)}, u32[]{:S(2)}) collective-permute-start(bf16[256,512]{1,0:T(8,128)(2,1)S(1)} %shard_map.115.refs_0_), channel_id=1, source_target_pairs={{0,512},{8,520},{16,528},{24,536},{32,544},{40,552},{48,560},{56,5... | collective-permute-start | bytes 786440 | tf_op jit(solution)/shard_map/ppermute | solution.py:29
  63.9 0.0 collective-permute-done.5.refs_0_
  63.9 0.0 collective-permute-done.6.refs_1_
  63.9 2.3 %collective-permute-start.7 = (bf16[256,512]{1,0:T(8,128)(2,1)S(1)}, bf16[256,512]{1,0:T(8,128)(2,1)S(1)}, u32[]{:S(2)}, u32[]{:S(2)}) collective-permute-start(bf16[256,512]{1,0:T(8,128)(2,1)S(1)} %shard_map.116.refs_1_), channel_id=1, source_target_pairs={{0,512},{8,520},{16,528},{24,536},{32,544},{40,552},{48,560},{56,5... | collective-permute-start | bytes 786440 | tf_op jit(solution)/shard_map/ppermute | solution.py:29
  66.2 0.0 copy-start.1
  66.3 0.0 copy-start.5
  66.3 4.6 %collective-permute-start.12 = (bf16[512,512]{1,0:T(8,128)(2,1)S(1)}, bf16[512,512]{1,0:T(8,128)(2,1)S(1)}, u32[]{:S(2)}, u32[]{:S(2)}) collective-permute-start(bf16[512,512]{1,0:T(8,128)(2,1)S(1)} %shard_map.118.refs_0_), channel_id=1, source_target_pairs={{0,16},{8,504},{16,32},{24,8},{32,48},{40,24},{48,64},{56,40},{64,... | collective-permute-start | bytes 1572872 | tf_op jit(solution)/shard_map/ppermute | solution.py:29
  70.8 0.0 collective-permute-done.4.refs_0_
  70.8 2.9 %collective-permute-done.7.refs_1_ = bf16[256,512]{1,0:T(8,128)(2,1)S(1)} collective-permute-done((bf16[256,512]{1,0:T(8,128)(2,1)S(1)}, bf16[256,512]{1,0:T(8,128)(2,1)S(1)}, u32[]{:S(2)}, u32[]{:S(2)}) %collective-permute-start.7) | collective-permute-done | bytes 262176 | tf_op jit(solution)/shard_map/ppermute | solution.py:29
  73.8 6.4 %collective-permute-start.9 = (bf16[512,512]{1,0:T(8,128)(2,1)S(1)}, bf16[512,512]{1,0:T(8,128)(2,1)S(1)}, u32[]{:S(2)}, u32[]{:S(2)}) collective-permute-start(bf16[512,512]{1,0:T(8,128)(2,1)S(1)} %shard_map.117.refs_0_), channel_id=1, source_target_pairs={{0,16},{8,504},{16,32},{24,8},{32,48},{40,24},{48,64},{56,40},{64,... | collective-permute-start | bytes 1572872 | tf_op jit(solution)/shard_map/ppermute | solution.py:29
  80.2 1.9 %collective-permute-start.11 = (bf16[512,512]{1,0:T(8,128)(2,1)S(1)}, bf16[512,512]{1,0:T(8,128)(2,1)S(1)}, u32[]{:S(2)}, u32[]{:S(2)}) collective-permute-start(bf16[512,512]{1,0:T(8,128)(2,1)S(1)} %shard_map.118.refs_0_), channel_id=1, source_target_pairs={{0,8},{8,0},{16,24},{24,16},{32,40},{40,32},{48,56},{56,48},{64,72... | collective-permute-start | bytes 1572872 | tf_op jit(solution)/shard_map/ppermute | solution.py:29
  82.1 0.0 collective-permute-done.12.refs_2_
  82.1 2.4 %collective-permute-start.13 = (bf16[512,512]{1,0:T(8,128)(2,1)S(1)}, bf16[512,512]{1,0:T(8,128)(2,1)S(1)}, u32[]{:S(2)}, u32[]{:S(2)}) collective-permute-start(bf16[512,512]{1,0:T(8,128)(2,1)S(1)} %collective-permute-done.12.refs_2_), channel_id=1, source_target_pairs={{0,8},{8,0},{16,24},{24,16},{32,40},{40,32},{48,56},{56,48},{64,72... | collective-permute-start | bytes 1572872 | tf_op jit(solution)/shard_map/ppermute | solution.py:29
  84.6 1.9 %collective-permute-start.8 = (bf16[512,512]{1,0:T(8,128)(2,1)S(1)}, bf16[512,512]{1,0:T(8,128)(2,1)S(1)}, u32[]{:S(2)}, u32[]{:S(2)}) collective-permute-start(bf16[512,512]{1,0:T(8,128)(2,1)S(1)} %shard_map.117.refs_0_), channel_id=1, source_target_pairs={{0,8},{8,0},{16,24},{24,16},{32,40},{40,32},{48,56},{56,48},{64,72... | collective-permute-start | bytes 1572872 | tf_op jit(solution)/shard_map/ppermute | solution.py:29
  86.5 0.0 collective-permute-done.9.refs_2_
  86.5 3.3 %collective-permute-start.10 = (bf16[512,512]{1,0:T(8,128)(2,1)S(1)}, bf16[512,512]{1,0:T(8,128)(2,1)S(1)}, u32[]{:S(2)}, u32[]{:S(2)}) collective-permute-start(bf16[512,512]{1,0:T(8,128)(2,1)S(1)} %collective-permute-done.9.refs_2_), channel_id=1, source_target_pairs={{0,8},{8,0},{16,24},{24,16},{32,40},{40,32},{48,56},{56,48},{64,72... | collective-permute-start | bytes 1572872 | tf_op jit(solution)/shard_map/ppermute | solution.py:29
  89.8 0.0 collective-permute-done.11.refs_1_
  89.8 0.0 collective-permute-done.13.refs_3_
  89.9 0.0 copy-done.1
  89.9 0.0 copy-done.5
  89.9 1.3 %shard_map.119 = (f32[128,512]{1,0:T(8,128)S(1)}, f32[128,2048]{1,0:T(8,128)S(1)}) custom-call(bf16[512,512]{1,0:T(8,128)(2,1)S(1)} %shard_map.118.refs_0_, bf16[512,512]{1,0:T(8,128)(2,1)S(1)} %collective-permute-done.11.refs_1_, bf16[512,512]{1,0:T(8,128)(2,1)S(1)} %collective-permute-done.12.refs_2_, ...), custom_call_target="tpu_custom_call" | custom-call | flops 536870912 | bytes 4194304 | tf_op jit(solution)/shard_map/pallas_call | solution.py:269
  91.2 0.0 collective-permute-done.8.refs_1_
  91.2 0.2 collective-permute-done.10.refs_3_
  91.4 2.8 %shard_map.120 = (bf16[128,512]{1,0:T(8,128)(2,1)}, bf16[128,4096]{1,0:T(8,128)(2,1)}) custom-call(bf16[512,512]{1,0:T(8,128)(2,1)S(1)} %shard_map.117.refs_0_, bf16[512,512]{1,0:T(8,128)(2,1)S(1)} %collective-permute-done.8.refs_1_, bf16[512,512]{1,0:T(8,128)(2,1)S(1)} %collective-permute-done.9.refs_2_, ...), custom_call_target="tpu_custom_call" | custom-call | flops 536870912 | bytes 4194304 | tf_op jit(solution)/shard_map/pallas_call | solution.py:281
  (6 shorter events, 0.1 us)
Async XLA Ops:
  0.6 20.6 %collective-permute-start.1 = (bf16[32,512]{1,0:T(8,128)(2,1)}, bf16[32,512]{1,0:T(8,128)(2,1)S(1)}, u32[]{:S(2)}, u32[]{:S(2)}) collective-permute-start(bf16[32,512]{1,0:T(8,128)(2,1)} %bitcast.16), channel_id=1, source_target_pairs={{0,0},{8,504},{16,16},{24,8},{32,32},{40,24},{48,48},{56,40},{64,6... | collective-permute-start | bytes 98312 | tf_op jit(solution)/shard_map/ppermute | solution.py:29
  19.9 3.6 %collective-permute-start = (bf16[32,512]{1,0:T(8,128)(2,1)}, bf16[32,512]{1,0:T(8,128)(2,1)S(1)}, u32[]{:S(2)}, u32[]{:S(2)}) collective-permute-start(bf16[32,512]{1,0:T(8,128)(2,1)} %bitcast.17), channel_id=1, source_target_pairs={{0,504},{8,0},{16,8},{24,16},{32,24},{40,32},{48,40},{56,48},{64,5... | collective-permute-start | bytes 98312 | tf_op jit(solution)/shard_map/ppermute | solution.py:29
  23.4 14.0 %collective-permute-start.2 = (bf16[64,512]{1,0:T(8,128)(2,1)S(1)}, bf16[64,512]{1,0:T(8,128)(2,1)S(1)}, u32[]{:S(2)}, u32[]{:S(2)}) collective-permute-start(bf16[64,512]{1,0:T(8,128)(2,1)S(1)} %shard_map.111.ahead.refs_0_), channel_id=1, source_target_pairs={{0,128},{8,392},{16,144},{24,408},{32,160},{40,424},{48,176},{56,4... | collective-permute-start | bytes 196616 | tf_op jit(solution)/shard_map/ppermute | solution.py:29
  32.2 1.0 %copy-start.2 = (f32[16,8192]{1,0:T(8,128)S(1)}, f32[16,8192]{1,0:T(8,128)}, u32[]{:S(2)}) copy-start(f32[16,8192]{1,0:T(8,128)} %params.1) | copy-start | bytes 1572868
  33.3 1.0 %copy-start.3 = (f32[1,16,8192]{2,1,0:T(8,128)S(1)}, f32[1,16,8192]{2,1,0:T(8,128)}, u32[]{:S(2)}) copy-start(f32[1,16,8192]{2,1,0:T(8,128)} %param.13) | copy-start | bytes 1572868
  34.3 1.0 %copy-start.4 = (f32[16,8192]{1,0:T(8,128)S(1)}, f32[16,8192]{1,0:T(8,128)}, u32[]{:S(2)}) copy-start(f32[16,8192]{1,0:T(8,128)} %momentum.1) | copy-start | bytes 1572868
  37.4 21.0 %copy-start = (bf16[1,128,4096]{2,1,0:T(8,128)(2,1)S(1)}, bf16[1,128,4096]{2,1,0:T(8,128)(2,1)}, u32[]{:S(2)}) copy-start(bf16[1,128,4096]{2,1,0:T(8,128)(2,1)} %param.8) | copy-start | bytes 3145732
  37.5 13.5 %collective-permute-start.3 = (bf16[128,512]{1,0:T(8,128)(2,1)S(1)}, bf16[128,512]{1,0:T(8,128)(2,1)S(1)}, u32[]{:S(2)}, u32[]{:S(2)}) collective-permute-start(bf16[128,512]{1,0:T(8,128)(2,1)S(1)} %shard_map.113.refs_0_), channel_id=1, source_target_pairs={{0,64},{8,456},{16,80},{24,472},{32,96},{40,488},{48,112},{56,504}... | collective-permute-start | bytes 393224 | tf_op jit(solution)/shard_map/ppermute | solution.py:29
  43.4 15.0 %all-to-all-start = ((f32[8,64,128]{2,1,0:T(8,128)}), f32[8,64,128]{2,1,0:T(8,128)S(1)}, u32[]{:S(2)}, u32[]{:S(2)}) async-start(f32[8,64,128]{2,1,0:T(8,128)} %get-tuple-element.14.refs_2_), calls=%async_computation | async-start | bytes 524288 | tf_op jit(solution)/shard_map/all_to_all | solution.py:243
  48.5 15.4 %collective-permute-start.5 = (bf16[128,512]{1,0:T(8,128)(2,1)S(1)}, bf16[128,512]{1,0:T(8,128)(2,1)S(1)}, u32[]{:S(2)}, u32[]{:S(2)}) collective-permute-start(bf16[128,512]{1,0:T(8,128)(2,1)S(1)} %shard_map.113.refs_0_), channel_id=1, source_target_pairs={{0,32},{8,488},{16,48},{24,504},{32,64},{40,8},{48,80},{56,24},{64... | collective-permute-start | bytes 393224 | tf_op jit(solution)/shard_map/ppermute | solution.py:29
  51.0 12.9 %collective-permute-start.6 = (bf16[128,512]{1,0:T(8,128)(2,1)S(1)}, bf16[128,512]{1,0:T(8,128)(2,1)S(1)}, u32[]{:S(2)}, u32[]{:S(2)}) collective-permute-start(bf16[128,512]{1,0:T(8,128)(2,1)S(1)} %collective-permute-done.3.refs_1_), channel_id=1, source_target_pairs={{0,32},{8,488},{16,48},{24,504},{32,64},{40,8},{48,80},{56,24},{64... | collective-permute-start | bytes 393224 | tf_op jit(solution)/shard_map/ppermute | solution.py:29
  59.3 11.5 %collective-permute-start.4 = (bf16[256,512]{1,0:T(8,128)(2,1)S(1)}, bf16[256,512]{1,0:T(8,128)(2,1)S(1)}, u32[]{:S(2)}, u32[]{:S(2)}) collective-permute-start(bf16[256,512]{1,0:T(8,128)(2,1)S(1)} %shard_map.115.refs_0_), channel_id=1, source_target_pairs={{0,512},{8,520},{16,528},{24,536},{32,544},{40,552},{48,560},{56,5... | collective-permute-start | bytes 786440 | tf_op jit(solution)/shard_map/ppermute | solution.py:29
  63.9 9.8 %collective-permute-start.7 = (bf16[256,512]{1,0:T(8,128)(2,1)S(1)}, bf16[256,512]{1,0:T(8,128)(2,1)S(1)}, u32[]{:S(2)}, u32[]{:S(2)}) collective-permute-start(bf16[256,512]{1,0:T(8,128)(2,1)S(1)} %shard_map.116.refs_1_), channel_id=1, source_target_pairs={{0,512},{8,520},{16,528},{24,536},{32,544},{40,552},{48,560},{56,5... | collective-permute-start | bytes 786440 | tf_op jit(solution)/shard_map/ppermute | solution.py:29
  66.2 23.6 %copy-start.1 = (bf16[1,128,512]{2,1,0:T(8,128)(2,1)S(1)}, bf16[1,128,512]{2,1,0:T(8,128)(2,1)}, u32[]{:S(2)}) copy-start(bf16[1,128,512]{2,1,0:T(8,128)(2,1)} %param.11) | copy-start | bytes 393220
  66.3 23.6 %copy-start.5 = (bf16[1,4096]{1,0:T(2,128)(2,1)S(1)}, bf16[1,4096]{1,0:T(2,128)(2,1)}, u32[]{:S(2)}) copy-start(bf16[1,4096]{1,0:T(2,128)(2,1)} %refs_6_.3) | copy-start | bytes 24580
  66.3 15.9 %collective-permute-start.12 = (bf16[512,512]{1,0:T(8,128)(2,1)S(1)}, bf16[512,512]{1,0:T(8,128)(2,1)S(1)}, u32[]{:S(2)}, u32[]{:S(2)}) collective-permute-start(bf16[512,512]{1,0:T(8,128)(2,1)S(1)} %shard_map.118.refs_0_), channel_id=1, source_target_pairs={{0,16},{8,504},{16,32},{24,8},{32,48},{40,24},{48,64},{56,40},{64,... | collective-permute-start | bytes 1572872 | tf_op jit(solution)/shard_map/ppermute | solution.py:29
  73.8 12.7 %collective-permute-start.9 = (bf16[512,512]{1,0:T(8,128)(2,1)S(1)}, bf16[512,512]{1,0:T(8,128)(2,1)S(1)}, u32[]{:S(2)}, u32[]{:S(2)}) collective-permute-start(bf16[512,512]{1,0:T(8,128)(2,1)S(1)} %shard_map.117.refs_0_), channel_id=1, source_target_pairs={{0,16},{8,504},{16,32},{24,8},{32,48},{40,24},{48,64},{56,40},{64,... | collective-permute-start | bytes 1572872 | tf_op jit(solution)/shard_map/ppermute | solution.py:29
  80.2 9.6 %collective-permute-start.11 = (bf16[512,512]{1,0:T(8,128)(2,1)S(1)}, bf16[512,512]{1,0:T(8,128)(2,1)S(1)}, u32[]{:S(2)}, u32[]{:S(2)}) collective-permute-start(bf16[512,512]{1,0:T(8,128)(2,1)S(1)} %shard_map.118.refs_0_), channel_id=1, source_target_pairs={{0,8},{8,0},{16,24},{24,16},{32,40},{40,32},{48,56},{56,48},{64,72... | collective-permute-start | bytes 1572872 | tf_op jit(solution)/shard_map/ppermute | solution.py:29
  82.1 7.7 %collective-permute-start.13 = (bf16[512,512]{1,0:T(8,128)(2,1)S(1)}, bf16[512,512]{1,0:T(8,128)(2,1)S(1)}, u32[]{:S(2)}, u32[]{:S(2)}) collective-permute-start(bf16[512,512]{1,0:T(8,128)(2,1)S(1)} %collective-permute-done.12.refs_2_), channel_id=1, source_target_pairs={{0,8},{8,0},{16,24},{24,16},{32,40},{40,32},{48,56},{56,48},{64,72... | collective-permute-start | bytes 1572872 | tf_op jit(solution)/shard_map/ppermute | solution.py:29
  84.6 6.6 %collective-permute-start.8 = (bf16[512,512]{1,0:T(8,128)(2,1)S(1)}, bf16[512,512]{1,0:T(8,128)(2,1)S(1)}, u32[]{:S(2)}, u32[]{:S(2)}) collective-permute-start(bf16[512,512]{1,0:T(8,128)(2,1)S(1)} %shard_map.117.refs_0_), channel_id=1, source_target_pairs={{0,8},{8,0},{16,24},{24,16},{32,40},{40,32},{48,56},{56,48},{64,72... | collective-permute-start | bytes 1572872 | tf_op jit(solution)/shard_map/ppermute | solution.py:29
  86.5 4.9 %collective-permute-start.10 = (bf16[512,512]{1,0:T(8,128)(2,1)S(1)}, bf16[512,512]{1,0:T(8,128)(2,1)S(1)}, u32[]{:S(2)}, u32[]{:S(2)}) collective-permute-start(bf16[512,512]{1,0:T(8,128)(2,1)S(1)} %collective-permute-done.9.refs_2_), channel_id=1, source_target_pairs={{0,8},{8,0},{16,24},{24,16},{32,40},{40,32},{48,56},{56,48},{64,72... | collective-permute-start | bytes 1572872 | tf_op jit(solution)/shard_map/ppermute | solution.py:29
